TPU v7x, 256 devices: a whole 4x4x8 slice. The times are simulated.
256 devices in a mesh: lat: 8 (over x, core), lon: 32 (over z, y).
Axes of the slice: x: 4, y: 4, z: 8, core: 2. Of those that a mesh axis runs over, the one named last changes fastest.
Arguments:
- fields: bfloat16 [4, 32, 288, 1024], P(None, 'lat', 'lon'), may hold values from -6 to 6
- conv_first: float32 [9, 1024], replicated, may hold values from -2 to 2
- w_qkv: bfloat16 [1024, 3072], replicated, may hold values from -2 to 2
- w_out: bfloat16 [1024, 1024], replicated, may hold values from -0.1875 to 0.1875
- conv_second: float32 [9, 1024], replicated, may hold values from -2 to 2
- key_list: int32 [8, 32, 32], P('lat', 'lon'), may hold values from 0 to 31, as said below
- key_count: int32 [8, 32], P('lat', 'lon'), may hold values from 1 to 32, as said below
Outputs:
- attended: bfloat16 [4, 32, 288, 1024], P(None, 'lat', 'lon')
- mixed: bfloat16 [4, 32, 288, 1024], P(None, 'lat', 'lon')
Inputs may be any that keep to these rules, and one draw needn't show every extreme that they name: Entry 0 of key_list[p, q] is q; entries 1 to key_count[p, q] - 1 are distinct longitude band indices other than q; the remaining entries are q. key_count[p, q] is 32 in the first and the last latitude band.
All inputs are finite; a program needn't handle non-finite values.
Results may differ from a plain program's by a relative error of at most 0.034.
Values may be sent and summed in bfloat16 or wider, within the bound.
A program may use at most 128 MiB of HBM per device.

v0:
```python
import jax
import jax.numpy as jnp
from jax import lax
from jax.sharding import PartitionSpec as P

HEADS = 16


NEG_FILL = -1e30
EPSILON = 1e-05


def with_halo(cells, sides, width, closed):
    for axis, dim in sides:
        count = lax.axis_size(axis)
        ends = count if closed else count - 1
        head = lax.slice_in_dim(cells, 0, width, axis=dim)
        tail = lax.slice_in_dim(cells, cells.shape[dim] - width, cells.shape[dim], axis=dim)
        cells = jnp.concatenate(
            [
                lax.ppermute(tail, axis, [(i, (i + 1) % count) for i in range(ends)]),
                cells,
                lax.ppermute(head, axis, [((i + 1) % count, i) for i in range(ends)]),
            ],
            axis=dim,
        )
    return cells


def from_behind(x, axis, by):
    size = lax.axis_size(axis)
    return lax.ppermute(x, axis, [(i, (i + by) % size) for i in range(size)])


def depthwise(field, weights):
    row_count = field.shape[1]
    column_count = field.shape[2]
    widened = with_halo(field, (("lon", 2),), 1, True)
    widened = with_halo(widened, (("lat", 1),), 1, False)
    result = jnp.zeros(field.shape, jnp.float32)
    for offset_lat in range(3):
        for offset_lon in range(3):
            window = widened[
                :, offset_lat : offset_lat + row_count, offset_lon : offset_lon + column_count
            ]
            result = result + weights[3 * offset_lat + offset_lon] * window.astype(jnp.float32)
    return result


def attend(state, query, keyvals, valid, scale):
    highest, summed, accum = state
    width = keyvals.shape[1] // 2
    heads = query.shape[1]
    head_size = query.shape[2]
    keys_part = keyvals[:, :width].reshape(-1, heads, head_size)
    values_part = keyvals[:, width:].reshape(-1, heads, head_size)
    scores = (
        jnp.einsum("qhd,khd->qhk", query, keys_part, preferred_element_type=jnp.float32) * scale
    )
    scores = jnp.where(valid[None, None, :], scores, NEG_FILL)
    new_highest = jnp.maximum(highest, jnp.max(scores, axis=-1))
    weights = jnp.where(valid[None, None, :], jnp.exp(scores - new_highest[..., None]), 0.0)
    factor = jnp.exp(highest - new_highest)
    summed = summed * factor + jnp.sum(weights, axis=-1)
    accum = accum * factor[..., None] + jnp.einsum(
        "qhk,khd->qhd",
        weights.astype(jnp.bfloat16),
        values_part,
        preferred_element_type=jnp.float32,
    )
    return (new_highest, summed, accum)


def local(fields, conv_first, w_qkv, w_out, conv_second, key_list, key_count):
    level_count, row_count, column_count, width = fields.shape
    tokens = level_count * row_count * column_count
    heads = HEADS
    head_size = width // heads
    scale = head_size ** (-0.5)
    stream = (fields.astype(jnp.float32) + depthwise(fields, conv_first)).astype(jnp.bfloat16)
    stream_flat = stream.reshape(tokens, width).astype(jnp.float32)
    normed = (
        stream_flat
        * lax.rsqrt(jnp.mean(stream_flat * stream_flat, axis=-1, keepdims=True) + EPSILON)
    ).astype(jnp.bfloat16)
    query = (
        jnp.dot(normed, w_qkv[:, :width], preferred_element_type=jnp.float32)
        .astype(jnp.bfloat16)
        .reshape(tokens, heads, head_size)
    )
    w_pair = w_qkv[:, width:]
    keyvals = jnp.dot(normed, w_pair, preferred_element_type=jnp.float32).astype(jnp.bfloat16)
    lat_here = lax.axis_index("lat")
    lat_total = lax.axis_size("lat")
    lon_here = lax.axis_index("lon")
    lon_total = lax.axis_size("lon")
    slot_index = jnp.arange(lon_total, dtype=jnp.int32)
    listed = key_list.reshape(lon_total)
    count = key_count.reshape(())
    linked = jnp.any(
        (listed[None, :] == slot_index[:, None]) & (slot_index < count)[None, :], axis=1
    )

    def spread(flag):
        return jnp.broadcast_to(flag, (tokens,))

    grid = keyvals.reshape(level_count, row_count, column_count, keyvals.shape[1])
    band = with_halo(grid, (("lat", 1),), row_count, False)
    upper = band[:, :row_count].reshape(tokens, keyvals.shape[1])
    lower = band[:, 2 * row_count :].reshape(tokens, keyvals.shape[1])
    near_keys = jnp.concatenate([upper, keyvals, lower], axis=0)
    near_valid = jnp.concatenate(
        [spread(lat_here > 0), jnp.ones((tokens,), jnp.bool_), spread(lat_here < lat_total - 1)]
    )
    state = (
        jnp.full((tokens, heads), NEG_FILL, jnp.float32),
        jnp.zeros((tokens, heads), jnp.float32),
        jnp.zeros((tokens, heads, head_size), jnp.float32),
    )
    state = attend(state, query, near_keys, near_valid, scale)

    def visit(current, piece, valid):
        return attend(current, query, piece, valid, scale)

    def turn(step, carry):
        buffer, current = carry
        buffer = from_behind(buffer, "lon", 1)
        source = (lon_here - step) % lon_total
        return (buffer, visit(current, buffer, spread(linked[source])))

    state = lax.fori_loop(1, lon_total, turn, (keyvals, state))[1]
    highest, summed, accum = state
    attended = (accum / summed[..., None]).astype(jnp.bfloat16).reshape(tokens, width)
    projected = jnp.dot(attended, w_out, preferred_element_type=jnp.float32)
    after = (stream_flat + projected).astype(jnp.bfloat16).reshape(fields.shape)
    mixed = (after.astype(jnp.float32) + depthwise(after, conv_second)).astype(jnp.bfloat16)
    return (attended.reshape(fields.shape), mixed)


def solution(mesh):
    return jax.shard_map(
        local,
        mesh=mesh,
        in_specs=(
            P(None, "lat", "lon", None),
            P(),
            P(),
            P(),
            P(),
            P("lat", "lon", None),
            P("lat", "lon"),
        ),
        out_specs=(P(None, "lat", "lon", None), P(None, "lat", "lon", None)),
        check_vma=False,
    )
```

profile of v0, /device:TPU:1, one launch (start us, length us, event | category | flops | bytes accessed | tf_op | source)
XLA Modules:
  0.0 842.3 jit_solution(13573127787496812850)
XLA Ops:
  3.8 6.8 collective-permute-start.2
  13.2 4.5 collective-permute-start.3
  21.5 3.1 collective-permute-done.4
  24.6 4.1 multiply_reduce_fusion
  31.7 3.0 fusion.21
  35.9 2.6 copy.84
  40.4 3.4 collective-permute-start.6
  44.1 2.8 fusion.37
  64.3 4.9 fusion.33
  69.3 715.7 %while.21 = (s32[]{:T(128)}, bf16[144,2048]{1,0:T(8,128)(2,1)S(1)}, f32[144,16]{0,1:T(8,128)S(1)}, f32[144,16]{0,1:T(8,128)S(1)}, f32[144,16,64]{0,2,1:T(8,128)}...) while((s32[]{:T(128)}, bf16[144,2048]{1,0:T(8,128)(2,1)S(1)}, ...), condition=%wide.region_7.8_spmd, body=%wide.region_4.7_spmd.sunk | while | flops 89547280 | bytes 17990036 | solution.py:131
  69.9 17.2 %collective-permute-done = bf16[144,2048]{1,0:T(8,128)(2,1)S(1)} collective-permute-done((bf16[144,2048]{1,0:T(8,128)(2,1)S(1)}, bf16[144,2048]{1,0:T(8,128)(2,1)S(1)}, u32[]{:S(2)}, u32[]{:S(2)}) %collective-permute-start) | collective-permute-done | bytes 589856 | tf_op jit(solution)/shard_map/while/body/eval_jaxpr/ppermute | solution.py:32
  96.4 17.5 %collective-permute-done = bf16[144,2048]{1,0:T(8,128)(2,1)S(1)} collective-permute-done((bf16[144,2048]{1,0:T(8,128)(2,1)S(1)}, bf16[144,2048]{1,0:T(8,128)(2,1)S(1)}, u32[]{:S(2)}, u32[]{:S(2)}) %collective-permute-start) | collective-permute-done | bytes 589856 | tf_op jit(solution)/shard_map/while/body/eval_jaxpr/ppermute | solution.py:32
  123.3 16.6 %collective-permute-done = bf16[144,2048]{1,0:T(8,128)(2,1)S(1)} collective-permute-done((bf16[144,2048]{1,0:T(8,128)(2,1)S(1)}, bf16[144,2048]{1,0:T(8,128)(2,1)S(1)}, u32[]{:S(2)}, u32[]{:S(2)}) %collective-permute-start) | collective-permute-done | bytes 589856 | tf_op jit(solution)/shard_map/while/body/eval_jaxpr/ppermute | solution.py:32
  149.3 15.7 %collective-permute-done = bf16[144,2048]{1,0:T(8,128)(2,1)S(1)} collective-permute-done((bf16[144,2048]{1,0:T(8,128)(2,1)S(1)}, bf16[144,2048]{1,0:T(8,128)(2,1)S(1)}, u32[]{:S(2)}, u32[]{:S(2)}) %collective-permute-start) | collective-permute-done | bytes 589856 | tf_op jit(solution)/shard_map/while/body/eval_jaxpr/ppermute | solution.py:32
  174.3 14.8 %collective-permute-done = bf16[144,2048]{1,0:T(8,128)(2,1)S(1)} collective-permute-done((bf16[144,2048]{1,0:T(8,128)(2,1)S(1)}, bf16[144,2048]{1,0:T(8,128)(2,1)S(1)}, u32[]{:S(2)}, u32[]{:S(2)}) %collective-permute-start) | collective-permute-done | bytes 589856 | tf_op jit(solution)/shard_map/while/body/eval_jaxpr/ppermute | solution.py:32
  198.5 13.8 %collective-permute-done = bf16[144,2048]{1,0:T(8,128)(2,1)S(1)} collective-permute-done((bf16[144,2048]{1,0:T(8,128)(2,1)S(1)}, bf16[144,2048]{1,0:T(8,128)(2,1)S(1)}, u32[]{:S(2)}, u32[]{:S(2)}) %collective-permute-start) | collective-permute-done | bytes 589856 | tf_op jit(solution)/shard_map/while/body/eval_jaxpr/ppermute | solution.py:32
  221.7 12.9 %collective-permute-done = bf16[144,2048]{1,0:T(8,128)(2,1)S(1)} collective-permute-done((bf16[144,2048]{1,0:T(8,128)(2,1)S(1)}, bf16[144,2048]{1,0:T(8,128)(2,1)S(1)}, u32[]{:S(2)}, u32[]{:S(2)}) %collective-permute-start) | collective-permute-done | bytes 589856 | tf_op jit(solution)/shard_map/while/body/eval_jaxpr/ppermute | solution.py:32
  244.0 12.0 %collective-permute-done = bf16[144,2048]{1,0:T(8,128)(2,1)S(1)} collective-permute-done((bf16[144,2048]{1,0:T(8,128)(2,1)S(1)}, bf16[144,2048]{1,0:T(8,128)(2,1)S(1)}, u32[]{:S(2)}, u32[]{:S(2)}) %collective-permute-start) | collective-permute-done | bytes 589856 | tf_op jit(solution)/shard_map/while/body/eval_jaxpr/ppermute | solution.py:32
  265.4 11.5 %collective-permute-done = bf16[144,2048]{1,0:T(8,128)(2,1)S(1)} collective-permute-done((bf16[144,2048]{1,0:T(8,128)(2,1)S(1)}, bf16[144,2048]{1,0:T(8,128)(2,1)S(1)}, u32[]{:S(2)}, u32[]{:S(2)}) %collective-permute-start) | collective-permute-done | bytes 589856 | tf_op jit(solution)/shard_map/while/body/eval_jaxpr/ppermute | solution.py:32
  279.8 2.3 bitcast_reduce_fusion.3
  286.2 11.5 %collective-permute-done = bf16[144,2048]{1,0:T(8,128)(2,1)S(1)} collective-permute-done((bf16[144,2048]{1,0:T(8,128)(2,1)S(1)}, bf16[144,2048]{1,0:T(8,128)(2,1)S(1)}, u32[]{:S(2)}, u32[]{:S(2)}) %collective-permute-start) | collective-permute-done | bytes 589856 | tf_op jit(solution)/shard_map/while/body/eval_jaxpr/ppermute | solution.py:32
  307.0 11.5 %collective-permute-done = bf16[144,2048]{1,0:T(8,128)(2,1)S(1)} collective-permute-done((bf16[144,2048]{1,0:T(8,128)(2,1)S(1)}, bf16[144,2048]{1,0:T(8,128)(2,1)S(1)}, u32[]{:S(2)}, u32[]{:S(2)}) %collective-permute-start) | collective-permute-done | bytes 589856 | tf_op jit(solution)/shard_map/while/body/eval_jaxpr/ppermute | solution.py:32
  327.9 11.5 %collective-permute-done = bf16[144,2048]{1,0:T(8,128)(2,1)S(1)} collective-permute-done((bf16[144,2048]{1,0:T(8,128)(2,1)S(1)}, bf16[144,2048]{1,0:T(8,128)(2,1)S(1)}, u32[]{:S(2)}, u32[]{:S(2)}) %collective-permute-start) | collective-permute-done | bytes 589856 | tf_op jit(solution)/shard_map/while/body/eval_jaxpr/ppermute | solution.py:32
  348.7 11.5 %collective-permute-done = bf16[144,2048]{1,0:T(8,128)(2,1)S(1)} collective-permute-done((bf16[144,2048]{1,0:T(8,128)(2,1)S(1)}, bf16[144,2048]{1,0:T(8,128)(2,1)S(1)}, u32[]{:S(2)}, u32[]{:S(2)}) %collective-permute-start) | collective-permute-done | bytes 589856 | tf_op jit(solution)/shard_map/while/body/eval_jaxpr/ppermute | solution.py:32
  363.1 2.3 bitcast_reduce_fusion.3
  369.6 11.5 %collective-permute-done = bf16[144,2048]{1,0:T(8,128)(2,1)S(1)} collective-permute-done((bf16[144,2048]{1,0:T(8,128)(2,1)S(1)}, bf16[144,2048]{1,0:T(8,128)(2,1)S(1)}, u32[]{:S(2)}, u32[]{:S(2)}) %collective-permute-start) | collective-permute-done | bytes 589856 | tf_op jit(solution)/shard_map/while/body/eval_jaxpr/ppermute | solution.py:32
  384.0 2.3 bitcast_reduce_fusion.3
  390.4 11.5 %collective-permute-done = bf16[144,2048]{1,0:T(8,128)(2,1)S(1)} collective-permute-done((bf16[144,2048]{1,0:T(8,128)(2,1)S(1)}, bf16[144,2048]{1,0:T(8,128)(2,1)S(1)}, u32[]{:S(2)}, u32[]{:S(2)}) %collective-permute-start) | collective-permute-done | bytes 589856 | tf_op jit(solution)/shard_map/while/body/eval_jaxpr/ppermute | solution.py:32
  411.3 11.5 %collective-permute-done = bf16[144,2048]{1,0:T(8,128)(2,1)S(1)} collective-permute-done((bf16[144,2048]{1,0:T(8,128)(2,1)S(1)}, bf16[144,2048]{1,0:T(8,128)(2,1)S(1)}, u32[]{:S(2)}, u32[]{:S(2)}) %collective-permute-start) | collective-permute-done | bytes 589856 | tf_op jit(solution)/shard_map/while/body/eval_jaxpr/ppermute | solution.py:32
  432.1 11.9 %collective-permute-done = bf16[144,2048]{1,0:T(8,128)(2,1)S(1)} collective-permute-done((bf16[144,2048]{1,0:T(8,128)(2,1)S(1)}, bf16[144,2048]{1,0:T(8,128)(2,1)S(1)}, u32[]{:S(2)}, u32[]{:S(2)}) %collective-permute-start) | collective-permute-done | bytes 589856 | tf_op jit(solution)/shard_map/while/body/eval_jaxpr/ppermute | solution.py:32
  446.9 2.3 bitcast_reduce_fusion.3
  453.4 13.0 %collective-permute-done = bf16[144,2048]{1,0:T(8,128)(2,1)S(1)} collective-permute-done((bf16[144,2048]{1,0:T(8,128)(2,1)S(1)}, bf16[144,2048]{1,0:T(8,128)(2,1)S(1)}, u32[]{:S(2)}, u32[]{:S(2)}) %collective-permute-start) | collective-permute-done | bytes 589856 | tf_op jit(solution)/shard_map/while/body/eval_jaxpr/ppermute | solution.py:32
  475.7 14.1 %collective-permute-done = bf16[144,2048]{1,0:T(8,128)(2,1)S(1)} collective-permute-done((bf16[144,2048]{1,0:T(8,128)(2,1)S(1)}, bf16[144,2048]{1,0:T(8,128)(2,1)S(1)}, u32[]{:S(2)}, u32[]{:S(2)}) %collective-permute-start) | collective-permute-done | bytes 589856 | tf_op jit(solution)/shard_map/while/body/eval_jaxpr/ppermute | solution.py:32
  499.2 15.1 %collective-permute-done = bf16[144,2048]{1,0:T(8,128)(2,1)S(1)} collective-permute-done((bf16[144,2048]{1,0:T(8,128)(2,1)S(1)}, bf16[144,2048]{1,0:T(8,128)(2,1)S(1)}, u32[]{:S(2)}, u32[]{:S(2)}) %collective-permute-start) | collective-permute-done | bytes 589856 | tf_op jit(solution)/shard_map/while/body/eval_jaxpr/ppermute | solution.py:32
  523.7 16.2 %collective-permute-done = bf16[144,2048]{1,0:T(8,128)(2,1)S(1)} collective-permute-done((bf16[144,2048]{1,0:T(8,128)(2,1)S(1)}, bf16[144,2048]{1,0:T(8,128)(2,1)S(1)}, u32[]{:S(2)}, u32[]{:S(2)}) %collective-permute-start) | collective-permute-done | bytes 589856 | tf_op jit(solution)/shard_map/while/body/eval_jaxpr/ppermute | solution.py:32
  549.3 17.3 %collective-permute-done = bf16[144,2048]{1,0:T(8,128)(2,1)S(1)} collective-permute-done((bf16[144,2048]{1,0:T(8,128)(2,1)S(1)}, bf16[144,2048]{1,0:T(8,128)(2,1)S(1)}, u32[]{:S(2)}, u32[]{:S(2)}) %collective-permute-start) | collective-permute-done | bytes 589856 | tf_op jit(solution)/shard_map/while/body/eval_jaxpr/ppermute | solution.py:32
  575.9 17.4 %collective-permute-done = bf16[144,2048]{1,0:T(8,128)(2,1)S(1)} collective-permute-done((bf16[144,2048]{1,0:T(8,128)(2,1)S(1)}, bf16[144,2048]{1,0:T(8,128)(2,1)S(1)}, u32[]{:S(2)}, u32[]{:S(2)}) %collective-permute-start) | collective-permute-done | bytes 589856 | tf_op jit(solution)/shard_map/while/body/eval_jaxpr/ppermute | solution.py:32
  602.7 16.5 %collective-permute-done = bf16[144,2048]{1,0:T(8,128)(2,1)S(1)} collective-permute-done((bf16[144,2048]{1,0:T(8,128)(2,1)S(1)}, bf16[144,2048]{1,0:T(8,128)(2,1)S(1)}, u32[]{:S(2)}, u32[]{:S(2)}) %collective-permute-start) | collective-permute-done | bytes 589856 | tf_op jit(solution)/shard_map/while/body/eval_jaxpr/ppermute | solution.py:32
  628.6 15.5 %collective-permute-done = bf16[144,2048]{1,0:T(8,128)(2,1)S(1)} collective-permute-done((bf16[144,2048]{1,0:T(8,128)(2,1)S(1)}, bf16[144,2048]{1,0:T(8,128)(2,1)S(1)}, u32[]{:S(2)}, u32[]{:S(2)}) %collective-permute-start) | collective-permute-done | bytes 589856 | tf_op jit(solution)/shard_map/while/body/eval_jaxpr/ppermute | solution.py:32
  653.5 14.6 %collective-permute-done = bf16[144,2048]{1,0:T(8,128)(2,1)S(1)} collective-permute-done((bf16[144,2048]{1,0:T(8,128)(2,1)S(1)}, bf16[144,2048]{1,0:T(8,128)(2,1)S(1)}, u32[]{:S(2)}, u32[]{:S(2)}) %collective-permute-start) | collective-permute-done | bytes 589856 | tf_op jit(solution)/shard_map/while/body/eval_jaxpr/ppermute | solution.py:32
  677.5 13.7 %collective-permute-done = bf16[144,2048]{1,0:T(8,128)(2,1)S(1)} collective-permute-done((bf16[144,2048]{1,0:T(8,128)(2,1)S(1)}, bf16[144,2048]{1,0:T(8,128)(2,1)S(1)}, u32[]{:S(2)}, u32[]{:S(2)}) %collective-permute-start) | collective-permute-done | bytes 589856 | tf_op jit(solution)/shard_map/while/body/eval_jaxpr/ppermute | solution.py:32
  700.5 12.8 %collective-permute-done = bf16[144,2048]{1,0:T(8,128)(2,1)S(1)} collective-permute-done((bf16[144,2048]{1,0:T(8,128)(2,1)S(1)}, bf16[144,2048]{1,0:T(8,128)(2,1)S(1)}, u32[]{:S(2)}, u32[]{:S(2)}) %collective-permute-start) | collective-permute-done | bytes 589856 | tf_op jit(solution)/shard_map/while/body/eval_jaxpr/ppermute | solution.py:32
  722.7 11.8 %collective-permute-done = bf16[144,2048]{1,0:T(8,128)(2,1)S(1)} collective-permute-done((bf16[144,2048]{1,0:T(8,128)(2,1)S(1)}, bf16[144,2048]{1,0:T(8,128)(2,1)S(1)}, u32[]{:S(2)}, u32[]{:S(2)}) %collective-permute-start) | collective-permute-done | bytes 589856 | tf_op jit(solution)/shard_map/while/body/eval_jaxpr/ppermute | solution.py:32
  743.9 11.5 %collective-permute-done = bf16[144,2048]{1,0:T(8,128)(2,1)S(1)} collective-permute-done((bf16[144,2048]{1,0:T(8,128)(2,1)S(1)}, bf16[144,2048]{1,0:T(8,128)(2,1)S(1)}, u32[]{:S(2)}, u32[]{:S(2)}) %collective-permute-start) | collective-permute-done | bytes 589856 | tf_op jit(solution)/shard_map/while/body/eval_jaxpr/ppermute | solution.py:32
  764.7 11.5 %collective-permute-done = bf16[144,2048]{1,0:T(8,128)(2,1)S(1)} collective-permute-done((bf16[144,2048]{1,0:T(8,128)(2,1)S(1)}, bf16[144,2048]{1,0:T(8,128)(2,1)S(1)}, u32[]{:S(2)}, u32[]{:S(2)}) %collective-permute-start) | collective-permute-done | bytes 589856 | tf_op jit(solution)/shard_map/while/body/eval_jaxpr/ppermute | solution.py:32
  788.2 4.8 collective-permute-start.8
  795.4 33.9 %collective-permute-start.10 = (bf16[4,1,11,1024]{3,2,1,0:T(8,128)(2,1)}, bf16[4,1,11,1024]{3,2,1,0:T(8,128)(2,1)S(1)}, u32[]{:S(2)}, u32[]{:S(2)}) collective-permute-start(bf16[4,1,11,1024]{3,2,1,0:T(8,128)(2,1)} %get-tuple-element.291), channel_id=1, source_target_pairs={{32,0},{64,32},{96,64},{128,96},{160,128},{192,160},{224,192},{33,... | collective-permute-start | bytes 270344 | tf_op jit(solution)/shard_map/ppermute | solution.py:23
  829.4 3.5 collective-permute-start.9
  (634 shorter events, 326.1 us)
Async XLA Ops:
  0.6 785.7 %copy-start = (bf16[1024,1024]{1,0:T(8,128)(2,1)S(1)}, bf16[1024,1024]{1,0:T(8,128)(2,1)}, u32[]{:S(2)}) copy-start(bf16[1024,1024]{1,0:T(8,128)(2,1)} %param.12) | copy-start | bytes 6291460
  1.6 10.2 %collective-permute-start.1 = (bf16[4,4,1,1024]{3,1,2,0:T(4,128)(2,1)S(1)}, bf16[4,4,1,1024]{3,1,2,0:T(4,128)(2,1)S(1)}, u32[]{:S(2)}, u32[]{:S(2)}) collective-permute-start(bf16[4,4,1,1024]{3,1,2,0:T(4,128)(2,1)S(1)} %get-tuple-element.297), channel_id=1, source_target_pairs={{0,1},{1,2},{2,3},{3,4},{4,5},{5,6},{6,7},{7,8},{8,9},{9,10},{10,1... | collective-permute-start | bytes 98312 | tf_op jit(solution)/shard_map/ppermute | solution.py:21
  3.8 9.1 %collective-permute-start.2 = (bf16[4,4,1,1024]{3,1,2,0:T(4,128)(2,1)S(1)}, bf16[4,4,1,1024]{3,1,2,0:T(4,128)(2,1)S(1)}, u32[]{:S(2)}, u32[]{:S(2)}) collective-permute-start(bf16[4,4,1,1024]{3,1,2,0:T(4,128)(2,1)S(1)} %get-tuple-element.296), channel_id=1, source_target_pairs={{1,0},{2,1},{3,2},{4,3},{5,4},{6,5},{7,6},{8,7},{9,8},{10,9},{11,1... | collective-permute-start | bytes 98312 | tf_op jit(solution)/shard_map/ppermute | solution.py:23
  13.2 8.2 collective-permute-start.3
  17.8 6.8 collective-permute-start.4
  31.4 12.7 %copy-start.3 = (f32[144,1024]{1,0:T(8,128)}, f32[144,1024]{1,0:T(8,128)S(1)}, u32[]{:S(2)}) copy-start(f32[144,1024]{1,0:T(8,128)S(1)} %reshape.114) | copy-start | bytes 1769476
  34.7 12.2 %copy-start.5 = (bf16[144,2048]{1,0:T(8,128)(2,1)}, bf16[144,2048]{1,0:T(8,128)(2,1)S(1)}, u32[]{:S(2)}) copy-start(bf16[144,2048]{1,0:T(8,128)(2,1)S(1)} %fusion.21) | copy-start | bytes 1769476
  34.7 9.3 %copy-start.14 = (s32[1,1,32]{2,1,0:T(1,128)S(1)}, s32[1,1,32]{2,1,0:T(1,128)}, u32[]{:S(2)}) copy-start(s32[1,1,32]{2,1,0:T(1,128)} %param.14) | copy-start | bytes 388
  38.5 10.4 %collective-permute-start.5 = (bf16[4,4,9,2048]{3,1,2,0:T(4,128)(2,1)}, bf16[4,4,9,2048]{3,1,2,0:T(4,128)(2,1)}, u32[]{:S(2)}, u32[]{:S(2)}) collective-permute-start(bf16[4,4,9,2048]{3,1,2,0:T(4,128)(2,1)} %copy.84), channel_id=1, source_target_pairs={{0,32},{32,64},{64,96},{96,128},{128,160},{160,192},{192,224},{1,3... | collective-permute-start | bytes 1769480 | tf_op jit(solution)/shard_map/ppermute | solution.py:21
  40.4 11.5 %collective-permute-start.6 = (bf16[4,4,9,2048]{3,1,2,0:T(4,128)(2,1)}, bf16[4,4,9,2048]{3,1,2,0:T(4,128)(2,1)}, u32[]{:S(2)}, u32[]{:S(2)}) collective-permute-start(bf16[4,4,9,2048]{3,1,2,0:T(4,128)(2,1)} %copy.84), channel_id=1, source_target_pairs={{32,0},{64,32},{96,64},{128,96},{160,128},{192,160},{224,192},{33,... | collective-permute-start | bytes 1769480 | tf_op jit(solution)/shard_map/ppermute | solution.py:23
  64.3 4.9 copy-start.6
  69.3 17.7 %collective-permute-start = (bf16[144,2048]{1,0:T(8,128)(2,1)S(1)}, bf16[144,2048]{1,0:T(8,128)(2,1)S(1)}, u32[]{:S(2)}, u32[]{:S(2)}) collective-permute-start(bf16[144,2048]{1,0:T(8,128)(2,1)S(1)} %get-tuple-element.394), channel_id=1, source_target_pairs={{0,1},{1,2},{2,3},{3,4},{4,5},{5,6},{6,7},{7,8},{8,9},{9,10},{10,1... | collective-permute-start | bytes 1769480 | tf_op jit(solution)/shard_map/while/body/eval_jaxpr/ppermute | solution.py:32
  95.8 18.1 %collective-permute-start = (bf16[144,2048]{1,0:T(8,128)(2,1)S(1)}, bf16[144,2048]{1,0:T(8,128)(2,1)S(1)}, u32[]{:S(2)}, u32[]{:S(2)}) collective-permute-start(bf16[144,2048]{1,0:T(8,128)(2,1)S(1)} %get-tuple-element.394), channel_id=1, source_target_pairs={{0,1},{1,2},{2,3},{3,4},{4,5},{5,6},{6,7},{7,8},{8,9},{9,10},{10,1... | collective-permute-start | bytes 1769480 | tf_op jit(solution)/shard_map/while/body/eval_jaxpr/ppermute | solution.py:32
  122.7 17.2 %collective-permute-start = (bf16[144,2048]{1,0:T(8,128)(2,1)S(1)}, bf16[144,2048]{1,0:T(8,128)(2,1)S(1)}, u32[]{:S(2)}, u32[]{:S(2)}) collective-permute-start(bf16[144,2048]{1,0:T(8,128)(2,1)S(1)} %get-tuple-element.394), channel_id=1, source_target_pairs={{0,1},{1,2},{2,3},{3,4},{4,5},{5,6},{6,7},{7,8},{8,9},{9,10},{10,1... | collective-permute-start | bytes 1769480 | tf_op jit(solution)/shard_map/while/body/eval_jaxpr/ppermute | solution.py:32
  142.8 3.6 copy-start.7
  148.7 16.3 %collective-permute-start = (bf16[144,2048]{1,0:T(8,128)(2,1)S(1)}, bf16[144,2048]{1,0:T(8,128)(2,1)S(1)}, u32[]{:S(2)}, u32[]{:S(2)}) collective-permute-start(bf16[144,2048]{1,0:T(8,128)(2,1)S(1)} %get-tuple-element.394), channel_id=1, source_target_pairs={{0,1},{1,2},{2,3},{3,4},{4,5},{5,6},{6,7},{7,8},{8,9},{9,10},{10,1... | collective-permute-start | bytes 1769480 | tf_op jit(solution)/shard_map/while/body/eval_jaxpr/ppermute | solution.py:32
  173.8 15.4 %collective-permute-start = (bf16[144,2048]{1,0:T(8,128)(2,1)S(1)}, bf16[144,2048]{1,0:T(8,128)(2,1)S(1)}, u32[]{:S(2)}, u32[]{:S(2)}) collective-permute-start(bf16[144,2048]{1,0:T(8,128)(2,1)S(1)} %get-tuple-element.394), channel_id=1, source_target_pairs={{0,1},{1,2},{2,3},{3,4},{4,5},{5,6},{6,7},{7,8},{8,9},{9,10},{10,1... | collective-permute-start | bytes 1769480 | tf_op jit(solution)/shard_map/while/body/eval_jaxpr/ppermute | solution.py:32
  197.9 14.4 %collective-permute-start = (bf16[144,2048]{1,0:T(8,128)(2,1)S(1)}, bf16[144,2048]{1,0:T(8,128)(2,1)S(1)}, u32[]{:S(2)}, u32[]{:S(2)}) collective-permute-start(bf16[144,2048]{1,0:T(8,128)(2,1)S(1)} %get-tuple-element.394), channel_id=1, source_target_pairs={{0,1},{1,2},{2,3},{3,4},{4,5},{5,6},{6,7},{7,8},{8,9},{9,10},{10,1... | collective-permute-start | bytes 1769480 | tf_op jit(solution)/shard_map/while/body/eval_jaxpr/ppermute | solution.py:32
  221.1 13.5 %collective-permute-start = (bf16[144,2048]{1,0:T(8,128)(2,1)S(1)}, bf16[144,2048]{1,0:T(8,128)(2,1)S(1)}, u32[]{:S(2)}, u32[]{:S(2)}) collective-permute-start(bf16[144,2048]{1,0:T(8,128)(2,1)S(1)} %get-tuple-element.394), channel_id=1, source_target_pairs={{0,1},{1,2},{2,3},{3,4},{4,5},{5,6},{6,7},{7,8},{8,9},{9,10},{10,1... | collective-permute-start | bytes 1769480 | tf_op jit(solution)/shard_map/while/body/eval_jaxpr/ppermute | solution.py:32
  243.4 12.6 %collective-permute-start = (bf16[144,2048]{1,0:T(8,128)(2,1)S(1)}, bf16[144,2048]{1,0:T(8,128)(2,1)S(1)}, u32[]{:S(2)}, u32[]{:S(2)}) collective-permute-start(bf16[144,2048]{1,0:T(8,128)(2,1)S(1)} %get-tuple-element.394), channel_id=1, source_target_pairs={{0,1},{1,2},{2,3},{3,4},{4,5},{5,6},{6,7},{7,8},{8,9},{9,10},{10,1... | collective-permute-start | bytes 1769480 | tf_op jit(solution)/shard_map/while/body/eval_jaxpr/ppermute | solution.py:32
  264.8 12.1 %collective-permute-start = (bf16[144,2048]{1,0:T(8,128)(2,1)S(1)}, bf16[144,2048]{1,0:T(8,128)(2,1)S(1)}, u32[]{:S(2)}, u32[]{:S(2)}) collective-permute-start(bf16[144,2048]{1,0:T(8,128)(2,1)S(1)} %get-tuple-element.394), channel_id=1, source_target_pairs={{0,1},{1,2},{2,3},{3,4},{4,5},{5,6},{6,7},{7,8},{8,9},{9,10},{10,1... | collective-permute-start | bytes 1769480 | tf_op jit(solution)/shard_map/while/body/eval_jaxpr/ppermute | solution.py:32
  279.8 3.6 copy-start.7
  285.6 12.1 %collective-permute-start = (bf16[144,2048]{1,0:T(8,128)(2,1)S(1)}, bf16[144,2048]{1,0:T(8,128)(2,1)S(1)}, u32[]{:S(2)}, u32[]{:S(2)}) collective-permute-start(bf16[144,2048]{1,0:T(8,128)(2,1)S(1)} %get-tuple-element.394), channel_id=1, source_target_pairs={{0,1},{1,2},{2,3},{3,4},{4,5},{5,6},{6,7},{7,8},{8,9},{9,10},{10,1... | collective-permute-start | bytes 1769480 | tf_op jit(solution)/shard_map/while/body/eval_jaxpr/ppermute | solution.py:32
  306.5 12.1 %collective-permute-start = (bf16[144,2048]{1,0:T(8,128)(2,1)S(1)}, bf16[144,2048]{1,0:T(8,128)(2,1)S(1)}, u32[]{:S(2)}, u32[]{:S(2)}) collective-permute-start(bf16[144,2048]{1,0:T(8,128)(2,1)S(1)} %get-tuple-element.394), channel_id=1, source_target_pairs={{0,1},{1,2},{2,3},{3,4},{4,5},{5,6},{6,7},{7,8},{8,9},{9,10},{10,1... | collective-permute-start | bytes 1769480 | tf_op jit(solution)/shard_map/while/body/eval_jaxpr/ppermute | solution.py:32
  327.3 12.1 %collective-permute-start = (bf16[144,2048]{1,0:T(8,128)(2,1)S(1)}, bf16[144,2048]{1,0:T(8,128)(2,1)S(1)}, u32[]{:S(2)}, u32[]{:S(2)}) collective-permute-start(bf16[144,2048]{1,0:T(8,128)(2,1)S(1)} %get-tuple-element.394), channel_id=1, source_target_pairs={{0,1},{1,2},{2,3},{3,4},{4,5},{5,6},{6,7},{7,8},{8,9},{9,10},{10,1... | collective-permute-start | bytes 1769480 | tf_op jit(solution)/shard_map/while/body/eval_jaxpr/ppermute | solution.py:32
  348.1 12.1 %collective-permute-start = (bf16[144,2048]{1,0:T(8,128)(2,1)S(1)}, bf16[144,2048]{1,0:T(8,128)(2,1)S(1)}, u32[]{:S(2)}, u32[]{:S(2)}) collective-permute-start(bf16[144,2048]{1,0:T(8,128)(2,1)S(1)} %get-tuple-element.394), channel_id=1, source_target_pairs={{0,1},{1,2},{2,3},{3,4},{4,5},{5,6},{6,7},{7,8},{8,9},{9,10},{10,1... | collective-permute-start | bytes 1769480 | tf_op jit(solution)/shard_map/while/body/eval_jaxpr/ppermute | solution.py:32
  369.0 12.1 %collective-permute-start = (bf16[144,2048]{1,0:T(8,128)(2,1)S(1)}, bf16[144,2048]{1,0:T(8,128)(2,1)S(1)}, u32[]{:S(2)}, u32[]{:S(2)}) collective-permute-start(bf16[144,2048]{1,0:T(8,128)(2,1)S(1)} %get-tuple-element.394), channel_id=1, source_target_pairs={{0,1},{1,2},{2,3},{3,4},{4,5},{5,6},{6,7},{7,8},{8,9},{9,10},{10,1... | collective-permute-start | bytes 1769480 | tf_op jit(solution)/shard_map/while/body/eval_jaxpr/ppermute | solution.py:32
  389.8 12.1 %collective-permute-start = (bf16[144,2048]{1,0:T(8,128)(2,1)S(1)}, bf16[144,2048]{1,0:T(8,128)(2,1)S(1)}, u32[]{:S(2)}, u32[]{:S(2)}) collective-permute-start(bf16[144,2048]{1,0:T(8,128)(2,1)S(1)} %get-tuple-element.394), channel_id=1, source_target_pairs={{0,1},{1,2},{2,3},{3,4},{4,5},{5,6},{6,7},{7,8},{8,9},{9,10},{10,1... | collective-permute-start | bytes 1769480 | tf_op jit(solution)/shard_map/while/body/eval_jaxpr/ppermute | solution.py:32
  410.7 12.1 %collective-permute-start = (bf16[144,2048]{1,0:T(8,128)(2,1)S(1)}, bf16[144,2048]{1,0:T(8,128)(2,1)S(1)}, u32[]{:S(2)}, u32[]{:S(2)}) collective-permute-start(bf16[144,2048]{1,0:T(8,128)(2,1)S(1)} %get-tuple-element.394), channel_id=1, source_target_pairs={{0,1},{1,2},{2,3},{3,4},{4,5},{5,6},{6,7},{7,8},{8,9},{9,10},{10,1... | collective-permute-start | bytes 1769480 | tf_op jit(solution)/shard_map/while/body/eval_jaxpr/ppermute | solution.py:32
  431.5 12.5 %collective-permute-start = (bf16[144,2048]{1,0:T(8,128)(2,1)S(1)}, bf16[144,2048]{1,0:T(8,128)(2,1)S(1)}, u32[]{:S(2)}, u32[]{:S(2)}) collective-permute-start(bf16[144,2048]{1,0:T(8,128)(2,1)S(1)} %get-tuple-element.394), channel_id=1, source_target_pairs={{0,1},{1,2},{2,3},{3,4},{4,5},{5,6},{6,7},{7,8},{8,9},{9,10},{10,1... | collective-permute-start | bytes 1769480 | tf_op jit(solution)/shard_map/while/body/eval_jaxpr/ppermute | solution.py:32
  452.8 13.6 %collective-permute-start = (bf16[144,2048]{1,0:T(8,128)(2,1)S(1)}, bf16[144,2048]{1,0:T(8,128)(2,1)S(1)}, u32[]{:S(2)}, u32[]{:S(2)}) collective-permute-start(bf16[144,2048]{1,0:T(8,128)(2,1)S(1)} %get-tuple-element.394), channel_id=1, source_target_pairs={{0,1},{1,2},{2,3},{3,4},{4,5},{5,6},{6,7},{7,8},{8,9},{9,10},{10,1... | collective-permute-start | bytes 1769480 | tf_op jit(solution)/shard_map/while/body/eval_jaxpr/ppermute | solution.py:32
  475.1 14.6 %collective-permute-start = (bf16[144,2048]{1,0:T(8,128)(2,1)S(1)}, bf16[144,2048]{1,0:T(8,128)(2,1)S(1)}, u32[]{:S(2)}, u32[]{:S(2)}) collective-permute-start(bf16[144,2048]{1,0:T(8,128)(2,1)S(1)} %get-tuple-element.394), channel_id=1, source_target_pairs={{0,1},{1,2},{2,3},{3,4},{4,5},{5,6},{6,7},{7,8},{8,9},{9,10},{10,1... | collective-permute-start | bytes 1769480 | tf_op jit(solution)/shard_map/while/body/eval_jaxpr/ppermute | solution.py:32
  498.6 15.7 %collective-permute-start = (bf16[144,2048]{1,0:T(8,128)(2,1)S(1)}, bf16[144,2048]{1,0:T(8,128)(2,1)S(1)}, u32[]{:S(2)}, u32[]{:S(2)}) collective-permute-start(bf16[144,2048]{1,0:T(8,128)(2,1)S(1)} %get-tuple-element.394), channel_id=1, source_target_pairs={{0,1},{1,2},{2,3},{3,4},{4,5},{5,6},{6,7},{7,8},{8,9},{9,10},{10,1... | collective-permute-start | bytes 1769480 | tf_op jit(solution)/shard_map/while/body/eval_jaxpr/ppermute | solution.py:32
  523.1 16.8 %collective-permute-start = (bf16[144,2048]{1,0:T(8,128)(2,1)S(1)}, bf16[144,2048]{1,0:T(8,128)(2,1)S(1)}, u32[]{:S(2)}, u32[]{:S(2)}) collective-permute-start(bf16[144,2048]{1,0:T(8,128)(2,1)S(1)} %get-tuple-element.394), channel_id=1, source_target_pairs={{0,1},{1,2},{2,3},{3,4},{4,5},{5,6},{6,7},{7,8},{8,9},{9,10},{10,1... | collective-permute-start | bytes 1769480 | tf_op jit(solution)/shard_map/while/body/eval_jaxpr/ppermute | solution.py:32
  548.7 17.9 %collective-permute-start = (bf16[144,2048]{1,0:T(8,128)(2,1)S(1)}, bf16[144,2048]{1,0:T(8,128)(2,1)S(1)}, u32[]{:S(2)}, u32[]{:S(2)}) collective-permute-start(bf16[144,2048]{1,0:T(8,128)(2,1)S(1)} %get-tuple-element.394), channel_id=1, source_target_pairs={{0,1},{1,2},{2,3},{3,4},{4,5},{5,6},{6,7},{7,8},{8,9},{9,10},{10,1... | collective-permute-start | bytes 1769480 | tf_op jit(solution)/shard_map/while/body/eval_jaxpr/ppermute | solution.py:32
  575.4 18.0 %collective-permute-start = (bf16[144,2048]{1,0:T(8,128)(2,1)S(1)}, bf16[144,2048]{1,0:T(8,128)(2,1)S(1)}, u32[]{:S(2)}, u32[]{:S(2)}) collective-permute-start(bf16[144,2048]{1,0:T(8,128)(2,1)S(1)} %get-tuple-element.394), channel_id=1, source_target_pairs={{0,1},{1,2},{2,3},{3,4},{4,5},{5,6},{6,7},{7,8},{8,9},{9,10},{10,1... | collective-permute-start | bytes 1769480 | tf_op jit(solution)/shard_map/while/body/eval_jaxpr/ppermute | solution.py:32
  602.1 17.1 %collective-permute-start = (bf16[144,2048]{1,0:T(8,128)(2,1)S(1)}, bf16[144,2048]{1,0:T(8,128)(2,1)S(1)}, u32[]{:S(2)}, u32[]{:S(2)}) collective-permute-start(bf16[144,2048]{1,0:T(8,128)(2,1)S(1)} %get-tuple-element.394), channel_id=1, source_target_pairs={{0,1},{1,2},{2,3},{3,4},{4,5},{5,6},{6,7},{7,8},{8,9},{9,10},{10,1... | collective-permute-start | bytes 1769480 | tf_op jit(solution)/shard_map/while/body/eval_jaxpr/ppermute | solution.py:32
  628.0 16.1 %collective-permute-start = (bf16[144,2048]{1,0:T(8,128)(2,1)S(1)}, bf16[144,2048]{1,0:T(8,128)(2,1)S(1)}, u32[]{:S(2)}, u32[]{:S(2)}) collective-permute-start(bf16[144,2048]{1,0:T(8,128)(2,1)S(1)} %get-tuple-element.394), channel_id=1, source_target_pairs={{0,1},{1,2},{2,3},{3,4},{4,5},{5,6},{6,7},{7,8},{8,9},{9,10},{10,1... | collective-permute-start | bytes 1769480 | tf_op jit(solution)/shard_map/while/body/eval_jaxpr/ppermute | solution.py:32
  652.9 15.2 %collective-permute-start = (bf16[144,2048]{1,0:T(8,128)(2,1)S(1)}, bf16[144,2048]{1,0:T(8,128)(2,1)S(1)}, u32[]{:S(2)}, u32[]{:S(2)}) collective-permute-start(bf16[144,2048]{1,0:T(8,128)(2,1)S(1)} %get-tuple-element.394), channel_id=1, source_target_pairs={{0,1},{1,2},{2,3},{3,4},{4,5},{5,6},{6,7},{7,8},{8,9},{9,10},{10,1... | collective-permute-start | bytes 1769480 | tf_op jit(solution)/shard_map/while/body/eval_jaxpr/ppermute | solution.py:32
  676.9 14.3 %collective-permute-start = (bf16[144,2048]{1,0:T(8,128)(2,1)S(1)}, bf16[144,2048]{1,0:T(8,128)(2,1)S(1)}, u32[]{:S(2)}, u32[]{:S(2)}) collective-permute-start(bf16[144,2048]{1,0:T(8,128)(2,1)S(1)} %get-tuple-element.394), channel_id=1, source_target_pairs={{0,1},{1,2},{2,3},{3,4},{4,5},{5,6},{6,7},{7,8},{8,9},{9,10},{10,1... | collective-permute-start | bytes 1769480 | tf_op jit(solution)/shard_map/while/body/eval_jaxpr/ppermute | solution.py:32
  699.9 13.4 %collective-permute-start = (bf16[144,2048]{1,0:T(8,128)(2,1)S(1)}, bf16[144,2048]{1,0:T(8,128)(2,1)S(1)}, u32[]{:S(2)}, u32[]{:S(2)}) collective-permute-start(bf16[144,2048]{1,0:T(8,128)(2,1)S(1)} %get-tuple-element.394), channel_id=1, source_target_pairs={{0,1},{1,2},{2,3},{3,4},{4,5},{5,6},{6,7},{7,8},{8,9},{9,10},{10,1... | collective-permute-start | bytes 1769480 | tf_op jit(solution)/shard_map/while/body/eval_jaxpr/ppermute | solution.py:32
  722.1 12.4 %collective-permute-start = (bf16[144,2048]{1,0:T(8,128)(2,1)S(1)}, bf16[144,2048]{1,0:T(8,128)(2,1)S(1)}, u32[]{:S(2)}, u32[]{:S(2)}) collective-permute-start(bf16[144,2048]{1,0:T(8,128)(2,1)S(1)} %get-tuple-element.394), channel_id=1, source_target_pairs={{0,1},{1,2},{2,3},{3,4},{4,5},{5,6},{6,7},{7,8},{8,9},{9,10},{10,1... | collective-permute-start | bytes 1769480 | tf_op jit(solution)/shard_map/while/body/eval_jaxpr/ppermute | solution.py:32
  743.3 12.1 %collective-permute-start = (bf16[144,2048]{1,0:T(8,128)(2,1)S(1)}, bf16[144,2048]{1,0:T(8,128)(2,1)S(1)}, u32[]{:S(2)}, u32[]{:S(2)}) collective-permute-start(bf16[144,2048]{1,0:T(8,128)(2,1)S(1)} %get-tuple-element.394), channel_id=1, source_target_pairs={{0,1},{1,2},{2,3},{3,4},{4,5},{5,6},{6,7},{7,8},{8,9},{9,10},{10,1... | collective-permute-start | bytes 1769480 | tf_op jit(solution)/shard_map/while/body/eval_jaxpr/ppermute | solution.py:32
  764.2 12.1 %collective-permute-start = (bf16[144,2048]{1,0:T(8,128)(2,1)S(1)}, bf16[144,2048]{1,0:T(8,128)(2,1)S(1)}, u32[]{:S(2)}, u32[]{:S(2)}) collective-permute-start(bf16[144,2048]{1,0:T(8,128)(2,1)S(1)} %get-tuple-element.394), channel_id=1, source_target_pairs={{0,1},{1,2},{2,3},{3,4},{4,5},{5,6},{6,7},{7,8},{8,9},{9,10},{10,1... | collective-permute-start | bytes 1769480 | tf_op jit(solution)/shard_map/while/body/eval_jaxpr/ppermute | solution.py:32
  788.1 6.5 collective-permute-start.7
  788.2 6.4 collective-permute-start.8
  795.4 43.1 %collective-permute-start.10 = (bf16[4,1,11,1024]{3,2,1,0:T(8,128)(2,1)}, bf16[4,1,11,1024]{3,2,1,0:T(8,128)(2,1)S(1)}, u32[]{:S(2)}, u32[]{:S(2)}) collective-permute-start(bf16[4,1,11,1024]{3,2,1,0:T(8,128)(2,1)} %get-tuple-element.291), channel_id=1, source_target_pairs={{32,0},{64,32},{96,64},{128,96},{160,128},{192,160},{224,192},{33,... | collective-permute-start | bytes 270344 | tf_op jit(solution)/shard_map/ppermute | solution.py:23
  829.4 9.1 %collective-permute-start.9 = (bf16[4,1,11,1024]{3,2,1,0:T(8,128)(2,1)S(1)}, bf16[4,1,11,1024]{3,2,1,0:T(8,128)(2,1)}, u32[]{:S(2)}, u32[]{:S(2)}) collective-permute-start(bf16[4,1,11,1024]{3,2,1,0:T(8,128)(2,1)S(1)} %get-tuple-element.290), channel_id=1, source_target_pairs={{0,32},{32,64},{64,96},{96,128},{128,160},{160,192},{192,224},{1,3... | collective-permute-start | bytes 270344 | tf_op jit(solution)/shard_map/ppermute | solution.py:21
  (98 other events, 260.0 us)
where the time goes:
time: 846 us; the launch traced here: 842 us
  waiting for transfers between devices  431 us (51%)
  local copies, waits for them, and re-layouts  168 us (20%)
  matrix products  126 us (15%)
  starting transfers between devices  63.2 us (7%)
  other arithmetic  49.5 us (6%)
    ppermute x31, waiting for transfers between devices, from_behind(): return lax.ppermute(x, axis, [(i, (i + by) % size) for i in range(size)])  425 us
    dot_general x32, matrix products, attend(): jnp.einsum('qhd,khd->qhk', query, keys_part, preferred_element_type=jnp.f...  73.3 us
    slice x64, local copies, waits for them, and re-layouts, attend(): values_part = keyvals[:, width:].reshape(-1, heads, head_size)  57.2 us
    ppermute x5, starting transfers between devices, with_halo(): lax.ppermute(head, axis, [((i + 1) % count, i) for i in range(ends)])  50.9 us
    dot_general x32, matrix products, attend(): jnp.einsum('qhk,khd->qhd', weights.astype(jnp.bfloat16), values_part, pre...  45.4 us
    reduce_sum x32, other arithmetic, attend(): summed = summed * factor + jnp.sum(weights, axis=-1)  38.1 us
    slice x32, local copies, waits for them, and re-layouts, attend(): keys_part = keyvals[:, :width].reshape(-1, heads, head_size)  37.5 us
    while x248, local copies, waits for them, and re-layouts  30.4 us
  transfers between devices with their start and end apart: 41, of which 35 were waited for; matrix products, arithmetic and copies ran while one was open for 4% of the time, Pallas kernels for 0%

commit v1 on v0

v1 whole, which is shorter than its diff:
```python
import functools
import math

import jax
import jax.numpy as jnp
from jax import lax
from jax.experimental import pallas as pl
from jax.experimental.pallas import tpu as pltpu
from jax.sharding import PartitionSpec as P

LEVELS, ROWS, COLS = 4, 4, 9
TOK = LEVELS * ROWS * COLS
HEAD = 64
LANES = 128
MSG = 3 * TOK + 16
EPSILON = 1e-05
NEG = -1e30
LOW = -3e38
MESH = pl.DeviceIdType.MESH
F32, BF16 = jnp.float32, jnp.bfloat16

SIDES = (
    (-1, 0, 0, 48),
    (1, 0, 48, 48),
    (0, -1, 96, 16),
    (0, 1, 112, 16),
    (-1, -1, 128, 16),
    (-1, 1, 144, 16),
    (1, -1, 160, 16),
    (1, 1, 176, 16),
)
OPPOSITE = (1, 0, 3, 2, 7, 6, 5, 4)
HALO_ROWS = 192


def cells_of(a, b):
    rows = {-1: [1], 1: [ROWS], 0: list(range(1, ROWS + 1))}[a]
    cols = {-1: [1], 1: [COLS], 0: list(range(1, COLS + 1))}[b]
    rim = [(r, c) for r in rows for c in cols]
    return rim, [(r + a, c + b) for r, c in rim]


def kernel(
    nlat, nz, ny,
    fields, conv_a, conv_b, key_list, key_count, w_qkv, w_out,
    att_out, mix_out,
    wq, wo, flat, grid, stream, stage, halo_f, halo_send, halo_recv,
    send_buf, recv_buf, gath, near, qx, kx, vx, acc, top, back_send, back_recv,
    w_sem, hs_sem, hr_sem, zs_sem, zr_sem, ys_sem, yr_sem, rs_sem, rr_sem, ls_sem, lr_sem, bs_sem, br_sem,
):
    lat = lax.axis_index("lat")
    lon = lax.axis_index("lon")
    z = lon // ny
    y = lon % ny
    nlon = nz * ny
    width = nz * LANES
    has_north = lat > 0
    has_south = lat < nlat - 1

    def wrap(i, n):
        return lax.rem(i + n, n)

    def at(zz, yy):
        return (lat, zz * ny + yy)

    wq_copy = pltpu.make_async_copy(w_qkv, wq, w_sem.at[0])
    wo_copy = pltpu.make_async_copy(w_out, wo, w_sem.at[1])
    wq_copy.start()
    wo_copy.start()

    barrier = pltpu.get_barrier_semaphore()

    def greet(dev):
        pl.semaphore_signal(barrier, inc=1, device_id=dev, device_id_type=MESH)

    for k in range(1, nz):
        greet(at(wrap(z + k, nz), y))
    greet(at(z, wrap(y + 1, ny)))
    greet(at(z, wrap(y - 1, ny)))
    greet((lat, wrap(lon + 1, nlon)))
    greet((lat, wrap(lon - 1, nlon)))

    @pl.when(has_north)
    def _():
        for d in (-1, 0, 1):
            greet((lat - 1, wrap(lon + d, nlon)))

    @pl.when(has_south)
    def _():
        for d in (-1, 0, 1):
            greet((lat + 1, wrap(lon + d, nlon)))

    for l in range(LEVELS):
        for r in range(ROWS):
            cells = fields[l, r].astype(F32)
            for t in range(nz):
                flat[t, pl.ds((l * ROWS + r) * 16, COLS), :] = cells[:, t * LANES : (t + 1) * LANES]
    for r in range(ROWS):
        for c in range(COLS):
            for t in range(nz):
                grid[r + 1, c + 1, 0:LEVELS, t * LANES : (t + 1) * LANES] = flat[
                    t, pl.ds(r * 16 + c, LEVELS, stride=ROWS * 16), :
                ]

    def exists(a):
        return {-1: has_north, 0: None, 1: has_south}[a]

    def maybe(cond, fn):
        if cond is None:
            fn()
        else:
            pl.when(cond)(fn)

    def halo_copy(which, i):
        a, b, first, rows = SIDES[i]
        first_there = SIDES[OPPOSITE[i]][2]
        return pltpu.make_async_remote_copy(
            src_ref=halo_send.at[which, pl.ds(first, rows)],
            dst_ref=halo_recv.at[which, pl.ds(first_there, rows)],
            send_sem=hs_sem.at[which, i],
            recv_sem=hr_sem.at[which, OPPOSITE[i]],
            device_id=(lat + a, wrap(lon + b, nlon)),
            device_id_type=MESH,
        )

    def halo_wait(which, i):
        a, b, first, rows = SIDES[i]
        return pltpu.make_async_remote_copy(
            src_ref=halo_send.at[which, pl.ds(first, rows)],
            dst_ref=halo_recv.at[which, pl.ds(first, rows)],
            send_sem=hs_sem.at[which, i],
            recv_sem=hr_sem.at[which, i],
            device_id=(lat + a, wrap(lon + b, nlon)),
            device_id_type=MESH,
        )

    def halo_start(which):
        for i, (a, b, first, rows) in enumerate(SIDES):
            rim, _ = cells_of(a, b)
            for n, (r, c) in enumerate(rim):
                halo_f[pl.ds(first + 4 * n, 4), :] = grid[r, c, 0:LEVELS, :]
            halo_send[which, pl.ds(first, rows), :] = halo_f[pl.ds(first, rows), :].astype(BF16)
            maybe(exists(a), lambda: halo_copy(which, i).start())

    def halo_end(which):
        for i, (a, b, first, rows) in enumerate(SIDES):
            maybe(exists(a), lambda: halo_wait(which, i).wait_recv())
            halo_f[pl.ds(first, rows), :] = halo_recv[which, pl.ds(first, rows), :].astype(F32)
            _, beyond = cells_of(a, b)
            for n, (r, c) in enumerate(beyond):
                value = halo_f[pl.ds(first + 4 * n, 4), :]
                if a != 0:
                    value = jnp.where(exists(a), value, 0.0)
                grid[r, c, 0:LEVELS, :] = value

    def conv(weights, dst):
        chunk = min(256, width)
        for first in range(0, width, chunk):
            lanes = slice(first, first + chunk)
            w = weights[:, lanes]
            for r in range(ROWS):
                total = grid[r + 1, 1 : COLS + 1, 0:LEVELS, lanes]
                for a in range(3):
                    for b in range(3):
                        total = total + w[3 * a + b][None, None, :] * grid[r + a, b : b + COLS, 0:LEVELS, lanes]
                total = total.astype(BF16).astype(F32)
                for c in range(COLS):
                    for t in range(chunk // LANES):
                        dst[first // LANES + t, pl.ds((r * COLS + c) * LEVELS, LEVELS), :] = total[
                            c, :, t * LANES : (t + 1) * LANES
                        ]

    greetings = nz - 1 + 4 + 3 * has_north.astype(jnp.int32) + 3 * has_south.astype(jnp.int32)
    halo_f[...] = jnp.zeros_like(halo_f)
    pl.semaphore_wait(barrier, greetings)
    halo_start(0)

    lane = lax.broadcasted_iota(jnp.int32, (16, LANES), 1)
    count = key_count[0, 0]
    seen = ((lane == nlon) & has_north) | ((lane == nlon + 1) & has_south)
    for s in range(nlon):
        seen = seen | (lane == jnp.where(s < count, key_list[0, 0, s], -1))
    bias = jnp.where(seen, 0.0, NEG).astype(BF16)
    for k in range(nz):
        send_buf[k, pl.ds(3 * TOK, 16), :] = bias

    halo_end(0)
    conv(conv_a, stream)

    def tokens(ref):
        return jnp.concatenate([ref[t] for t in range(nz)], axis=1)

    def keep(ref, value):
        for t in range(nz):
            ref[t] = value[:, t * LANES : (t + 1) * LANES]

    x = tokens(stream)
    normed = (x * lax.rsqrt(jnp.mean(x * x, axis=-1, keepdims=True) + EPSILON)).astype(BF16)
    wq_copy.wait()

    def z_copy(k):
        there = wrap(z + k, nz)
        return pltpu.make_async_remote_copy(
            src_ref=send_buf.at[there],
            dst_ref=recv_buf.at[k],
            send_sem=zs_sem.at[k],
            recv_sem=zr_sem.at[k],
            device_id=at(there, y),
            device_id_type=MESH,
        )

    scale = HEAD ** -0.5 * math.log2(math.e)
    npair = nz // 2
    pair = z // 2
    order = [npair // 2] + [o for o in range(1, npair) if o != npair // 2] + [0]
    for off in order:
        j = wrap(pair + off, npair)
        for part in range(3):
            cols = pl.ds(pl.multiple_of(part * width + j * 256, 256), 256)
            res = jnp.dot(normed, wq[:, cols], preferred_element_type=F32)
            if part == 0:
                res = res * scale
            res = res.astype(BF16)
            send_buf[2 * j, pl.ds(part * TOK, TOK), :] = res[:, :LANES]
            send_buf[2 * j + 1, pl.ds(part * TOK, TOK), :] = res[:, LANES:]
        for half in range(2):
            k = wrap(2 * j + half - z, nz)

            @pl.when(k != 0)
            def _():
                z_copy(k).start()

    recv_buf[0] = send_buf[z]

    def y_copy(way, k):
        return pltpu.make_async_remote_copy(
            src_ref=recv_buf.at[k, pl.ds(TOK, 2 * TOK)],
            dst_ref=gath.at[way, k],
            send_sem=ys_sem.at[way, k],
            recv_sem=yr_sem.at[way, k],
            device_id=at(z, wrap(y + 1 - 2 * way, ny)),
            device_id_type=MESH,
        )

    def relay_copy(way, k):
        rows = pl.ds(way * TOK, TOK)
        return pltpu.make_async_remote_copy(
            src_ref=gath.at[way, k, rows],
            dst_ref=gath.at[2, k, rows],
            send_sem=rs_sem.at[way, k],
            recv_sem=rr_sem.at[way, k],
            device_id=at(z, wrap(y + 1 - 2 * way, ny)),
            device_id_type=MESH,
        )

    def lat_copy(way, k):
        return pltpu.make_async_remote_copy(
            src_ref=recv_buf.at[k, pl.ds(TOK, 2 * TOK)],
            dst_ref=near.at[1 - way, k],
            send_sem=ls_sem.at[way, k],
            recv_sem=lr_sem.at[1 - way, k],
            device_id=(lat - 1 + 2 * way, lon),
            device_id_type=MESH,
        )

    def lat_wait(side, k):
        return pltpu.make_async_remote_copy(
            src_ref=recv_buf.at[k, pl.ds(TOK, 2 * TOK)],
            dst_ref=near.at[side, k],
            send_sem=ls_sem.at[side, k],
            recv_sem=lr_sem.at[side, k],
            device_id=(lat - 1 + 2 * side, lon),
            device_id_type=MESH,
        )

    def forward(k, carry):
        @pl.when(k > 0)
        def _():
            z_copy(k).wait_recv()

        y_copy(0, k).start()
        y_copy(1, k).start()

        @pl.when(has_north)
        def _():
            lat_copy(0, k).start()

        @pl.when(has_south)
        def _():
            lat_copy(1, k).start()

        return carry

    lax.fori_loop(0, nz, forward, 0)

    lane_t = lax.broadcasted_iota(jnp.int32, (TOK, LANES), 1)

    def prepare(k, carry):
        q = recv_buf[k, pl.ds(0, TOK), :]
        b = jnp.concatenate([recv_buf[k, pl.ds(3 * TOK, 16), :]] * (TOK // 16), axis=0)
        zero = jnp.zeros_like(q)
        qx[k, pl.ds(0, TOK), 0:LANES] = jnp.where(lane_t < HEAD, q, zero)
        qx[k, pl.ds(TOK, TOK), 0:LANES] = jnp.where(lane_t < HEAD, zero, q)
        qx[k, pl.ds(0, TOK), LANES:] = b
        qx[k, pl.ds(TOK, TOK), LANES:] = b
        top[k] = jnp.full((2 * TOK, LANES), LOW, F32)
        acc[k] = jnp.zeros((2 * TOK, 2 * LANES), F32)
        return carry

    lax.fori_loop(0, nz, prepare, 0)

    def relay(k, carry):
        for way in range(2):
            y_copy(way, k).wait_recv()
            relay_copy(way, k).start()
        return carry

    lax.fori_loop(0, nz, relay, 0)

    ones = jnp.ones((TOK, LANES), BF16)

    def attend(k, keys, values):
        s = lax.dot_general(qx[k], keys, (((1,), (1,)), ((), ())), preferred_element_type=F32)
        old = top[k]
        new = jnp.maximum(old, jnp.max(s, axis=1, keepdims=True))
        p = jnp.exp2(s - new[:, :1]).astype(BF16)
        pv = jnp.dot(p, values, preferred_element_type=F32)
        factor = jnp.exp2(old - new)
        acc[k] = acc[k] * jnp.concatenate([factor, factor], axis=1) + pv
        top[k] = new

    def fill(n, number, block):
        rows = pl.ds(pl.multiple_of(n * TOK, 16), TOK)
        kx[rows, 0:LANES] = block[0]
        kx[rows, LANES:] = jnp.where(lane_t == number, 1.0, 0.0).astype(BF16)
        vx[rows, 0:LANES] = block[1]

    for n in range(nz):
        vx[pl.ds(n * TOK, TOK), LANES:] = ones

    def band(read, y0):
        def put(k, carry):
            fill(k, wrap(z - k, nz) * ny + y0, read(k))
            return carry

        lax.fori_loop(0, nz, put, 0)

        def step(k, carry):
            attend(k, kx[...], vx[...])
            return carry

        lax.fori_loop(0, nz, step, 0)

    band(lambda k: (recv_buf[k, pl.ds(TOK, TOK), :], recv_buf[k, pl.ds(2 * TOK, TOK), :]), y)
    for way in range(2):
        band(lambda k: (gath[way, k, pl.ds(0, TOK), :], gath[way, k, pl.ds(TOK, TOK), :]), wrap(y - 1 + 2 * way, ny))

    def relay_wait(k, carry):
        relay_copy(0, k).wait_recv()
        relay_copy(1, k).wait_recv()
        return carry

    lax.fori_loop(0, nz, relay_wait, 0)
    band(lambda k: (gath[2, k, pl.ds(0, TOK), :], gath[2, k, pl.ds(TOK, TOK), :]), wrap(y + 2, ny))

    def back_copy(k):
        there = wrap(z - k, nz)
        return pltpu.make_async_remote_copy(
            src_ref=back_send.at[k],
            dst_ref=back_recv.at[z],
            send_sem=bs_sem.at[k],
            recv_sem=br_sem.at[k],
            device_id=at(there, y),
            device_id_type=MESH,
        )

    def back_wait(k):
        there = wrap(z + k, nz)
        return pltpu.make_async_remote_copy(
            src_ref=back_send.at[k],
            dst_ref=back_recv.at[there],
            send_sem=bs_sem.at[k],
            recv_sem=br_sem.at[k],
            device_id=at(there, y),
            device_id_type=MESH,
        )

    def finish(k, carry):
        for side, cond in ((0, has_north), (1, has_south)):

            @pl.when(cond)
            def _():
                lat_wait(side, k).wait_recv()

            there = cond
            block = [jnp.where(there, near[side, k, pl.ds(i * TOK, TOK), :], jnp.zeros((TOK, LANES), BF16)) for i in range(2)]
            fill(side, nlon + side, block)
        attend(k, kx[pl.ds(0, 2 * TOK), :], vx[pl.ds(0, 2 * TOK), :])
        result = acc[k]
        result = result[:, :LANES] / result[:, LANES:]
        result = jnp.where(lane_t < HEAD, result[:TOK], result[TOK:]).astype(BF16)

        @pl.when(k == 0)
        def _():
            back_recv[z] = result

        @pl.when(k > 0)
        def _():
            back_send[k] = result
            back_copy(k).start()

        return carry

    lax.fori_loop(0, nz, finish, 0)
    for k in range(1, nz):
        back_wait(k).wait_recv()

    attended = jnp.concatenate([back_recv[k] for k in range(nz)], axis=1)
    wo_copy.wait()
    after = tokens(stream) + jnp.dot(attended, wo[...], preferred_element_type=F32)
    keep(stage, after.astype(BF16).astype(F32))
    for r in range(ROWS):
        for c in range(COLS):
            for t in range(nz):
                grid[r + 1, c + 1, 0:LEVELS, t * LANES : (t + 1) * LANES] = stage[
                    t, pl.ds((r * COLS + c) * LEVELS, LEVELS), :
                ]
    halo_start(1)
    keep(stage, attended.astype(F32))

    def leave(out):
        for l in range(LEVELS):
            for r in range(ROWS):
                for t in range(nz):
                    out[l, r, :, t * LANES : (t + 1) * LANES] = stage[
                        t, pl.ds(r * COLS * LEVELS + l, COLS, stride=LEVELS), :
                    ].astype(BF16)

    leave(att_out)
    halo_end(1)
    conv(conv_b, stage)
    leave(mix_out)

    for which in range(2):
        for i, (a, b, first, rows) in enumerate(SIDES):
            maybe(exists(a), lambda: halo_copy(which, i).wait_send())

    def sent(k, carry):
        @pl.when(k > 0)
        def _():
            z_copy(k).wait_send()
            back_copy(k).wait_send()

        for way in range(2):
            y_copy(way, k).wait_send()
            relay_copy(way, k).wait_send()

        @pl.when(has_north)
        def _():
            lat_copy(0, k).wait_send()

        @pl.when(has_south)
        def _():
            lat_copy(1, k).wait_send()

        return carry

    lax.fori_loop(0, nz, sent, 0)


def local(nlat, nz, ny, fields, conv_first, w_qkv, w_out, conv_second, key_list, key_count):
    width = fields.shape[-1]
    vmem = pl.BlockSpec(memory_space=pltpu.VMEM)
    smem = pl.BlockSpec(memory_space=pltpu.SMEM)
    hbm = pl.BlockSpec(memory_space=pl.ANY)
    dma = pltpu.SemaphoreType.DMA
    out = jax.ShapeDtypeStruct(fields.shape, BF16)
    return pl.pallas_call(
        functools.partial(kernel, nlat, nz, ny),
        out_shape=(out, out),
        in_specs=[vmem, vmem, vmem, smem, smem, hbm, hbm],
        out_specs=(vmem, vmem),
        scratch_shapes=[
            pltpu.VMEM(w_qkv.shape, BF16),
            pltpu.VMEM(w_out.shape, BF16),
            pltpu.VMEM((nz, LEVELS * ROWS * 16, LANES), F32),
            pltpu.VMEM((ROWS + 2, COLS + 2, 8, width), F32),
            pltpu.VMEM((nz, TOK, LANES), F32),
            pltpu.VMEM((nz, TOK, LANES), F32),
            pltpu.VMEM((HALO_ROWS, width), F32),
            pltpu.VMEM((2, HALO_ROWS, width), BF16),
            pltpu.VMEM((2, HALO_ROWS, width), BF16),
            pltpu.VMEM((nz, MSG, LANES), BF16),
            pltpu.VMEM((nz, MSG, LANES), BF16),
            pltpu.VMEM((3, nz, 2 * TOK, LANES), BF16),
            pltpu.VMEM((2, nz, 2 * TOK, LANES), BF16),
            pltpu.VMEM((nz, 2 * TOK, 2 * LANES), BF16),
            pltpu.VMEM((nz * TOK, 2 * LANES), BF16),
            pltpu.VMEM((nz * TOK, 2 * LANES), BF16),
            pltpu.VMEM((nz, 2 * TOK, 2 * LANES), F32),
            pltpu.VMEM((nz, 2 * TOK, LANES), F32),
            pltpu.VMEM((nz, TOK, LANES), BF16),
            pltpu.VMEM((nz, TOK, LANES), BF16),
            dma((2,)),
            dma((2, 8)),
            dma((2, 8)),
            dma((nz,)),
            dma((nz,)),
            dma((2, nz)),
            dma((2, nz)),
            dma((2, nz)),
            dma((2, nz)),
            dma((2, nz)),
            dma((2, nz)),
            dma((nz,)),
            dma((nz,)),
        ],
        compiler_params=pltpu.CompilerParams(
            collective_id=0, has_side_effects=True, vmem_limit_bytes=56 * 1024 * 1024
        ),
        name="block",
    )(fields, conv_first, conv_second, key_list, key_count, w_qkv, w_out)


def solution(mesh):
    nlat, nlon = mesh.shape["lat"], mesh.shape["lon"]
    nz = 8
    return jax.shard_map(
        functools.partial(local, nlat, nz, nlon // nz),
        mesh=mesh,
        in_specs=(
            P(None, "lat", "lon", None),
            P(),
            P(),
            P(),
            P(),
            P("lat", "lon", None),
            P("lat", "lon"),
        ),
        out_specs=(P(None, "lat", "lon", None), P(None, "lat", "lon", None)),
        check_vma=False,
    )
```

time: 846 us -> 120 us (0.14)
  waiting for transfers between devices: 431 us -> 0 us
  local copies, waits for them, and re-layouts: 168 us -> 5.88 us
  matrix products: 126 us -> 0 us
  Pallas kernels: 0 us -> 113 us
  starting transfers between devices: 63.2 us -> 0 us
  other arithmetic: 49.5 us -> 0 us
    ppermute x41 -> x0, waiting for transfers between devices: 431 us -> none  [the longest x31 425 us: from_behind(): return lax.ppermute(x, axis, [(i, (i + by) % size) for i in range(size)])]
    dot_general x67 -> x0, matrix products: 126 us -> none  [the longest x32 73.3 us: attend(): jnp.einsum('qhd,khd->qhk', query, keys_part, preferred_element_type=jnp.f...]
    pallas_call x0 -> x1, Pallas kernels: none -> 113 us  [local(): pl.pallas_call(functools.partial(kernel, nlat, nz, ny), out_shape=(out, o...]
    slice x101 -> x0, local copies, waits for them, and re-layouts: 98.7 us -> none  [the longest x64 57.2 us: attend(): values_part = keyvals[:, width:].reshape(-1, heads, head_size)]
    ppermute x41 -> x0, starting transfers between devices: 63.2 us -> none  [the longest x5 50.9 us: with_halo(): lax.ppermute(head, axis, [((i + 1) % count, i) for i in range(ends)])]
    reduce_sum x33 -> x0, other arithmetic: 42.2 us -> none  [the longest x32 38.1 us: attend(): summed = summed * factor + jnp.sum(weights, axis=-1)]
    while x248 -> x0, local copies, waits for them, and re-layouts: 30.4 us -> none
    dynamic_slice x31 -> x0, local copies, waits for them, and re-layouts: 18.2 us -> none  [turn(): return (buffer, visit(current, buffer, spread(linked[source])))]
  transfers between devices with their start and end apart: 41 -> 0, of which waited for: 35 -> 0; matrix products, arithmetic and copies ran while one was open for 4% -> 0% of each run, Pallas kernels for 0% -> 0%
where the time goes in v1:
time: 120 us
  Pallas kernels  113 us (94%)
  local copies, waits for them, and re-layouts  5.88 us (5%)
  between operations  1.29 us (1%)
    pallas_call x1, Pallas kernels, local(): pl.pallas_call(functools.partial(kernel, nlat, nz, ny), out_shape=(out, o...  113 us
    pallas_call x2, local copies, waits for them, and re-layouts, local(): pl.pallas_call(functools.partial(kernel, nlat, nz, ny), out_shape=(out, o...  4 us

profile of v1, /device:TPU:1, one launch (start us, length us, event | category | flops | bytes accessed | tf_op | source)
XLA Modules:
  0.0 120.1 jit_solution(16392277023428457422)
XLA Ops:
  1.3 1.9 %copy.9.fields = bf16[4,4,9,1024]{3,2,1,0:T(8,128)(2,1)} copy(bf16[4,4,9,1024]{3,1,2,0:T(4,128)(2,1)} %param.7) | data formatting | bytes 589824 | tf_op args[0]
  3.2 112.9 %block.1 = (bf16[4,4,9,1024]{3,2,1,0:T(8,128)(2,1)}, bf16[4,4,9,1024]{3,2,1,0:T(8,128)(2,1)}) custom-call(bf16[4,4,9,1024]{3,2,1,0:T(8,128)(2,1)} %copy.9.fields, f32[9,1024]{1,0:T(8,128)} %conv_a.1, f32[9,1024]{1,0:T(8,128)} %conv_b.1, s32[1,1,32]{2,1,0:T(1,128)} %key_list.1, s32[1,1]{1,0:T(1,128)S(6)} %copy.12.key_count, bf16[1024,3072]{1,0:T(8,128)(2,1)} %w_qkv.1, ...), custom_call_target="tpu_custom_call" | custom-call | tf_op jit(solution)/shard_map/block/pallas_call | solution.py:478
  116.1 2.0 %copy.10 = bf16[4,4,9,1024]{3,1,2,0:T(4,128)(2,1)} copy(bf16[4,4,9,1024]{3,2,1,0:T(8,128)(2,1)} %get-tuple-element.2) | data formatting | bytes 589824 | tf_op jit(solution)/shard_map/block/pallas_call | solution.py:478
  118.1 2.0 %copy.11 = bf16[4,4,9,1024]{3,1,2,0:T(4,128)(2,1)} copy(bf16[4,4,9,1024]{3,2,1,0:T(8,128)(2,1)} %get-tuple-element.3) | data formatting | bytes 589824 | tf_op jit(solution)/shard_map/block/pallas_call | solution.py:478

commit v2 on v1

v2 whole, which is shorter than its diff:
```python
import functools
import math

import jax
import jax.numpy as jnp
from jax import lax
from jax.experimental import pallas as pl
from jax.experimental.pallas import tpu as pltpu
from jax.sharding import PartitionSpec as P

LEVELS, ROWS, COLS = 4, 4, 9
TOK = LEVELS * ROWS * COLS
HEAD = 64
LANES = 128
CHUNK = 8 * TOK
EPSILON = 1e-05
NEG = -1e30
LOW = -3e38
MESH = pl.DeviceIdType.MESH
F32, BF16 = jnp.float32, jnp.bfloat16

SIDES = (
    (-1, 0, 0, 48),
    (1, 0, 48, 48),
    (0, -1, 96, 16),
    (0, 1, 112, 16),
    (-1, -1, 128, 16),
    (-1, 1, 144, 16),
    (1, -1, 160, 16),
    (1, 1, 176, 16),
)
OPPOSITE = (1, 0, 3, 2, 7, 6, 5, 4)
HALO_ROWS = 192


def cells_of(a, b):
    rows = {-1: [1], 1: [ROWS], 0: list(range(1, ROWS + 1))}[a]
    cols = {-1: [1], 1: [COLS], 0: list(range(1, COLS + 1))}[b]
    rim = [(r, c) for r in rows for c in cols]
    return rim, [(r + a, c + b) for r, c in rim]


def kernel(
    nlat, nz, ny,
    fields, conv_a, conv_b, key_list, key_count, w_qkv, w_out,
    att_out, mix_out,
    wq, wo, flat, grid, stream, stage, halo_f, halo_send, halo_recv,
    q_send, q_recv, kv_send, kv, near, qx, kt, vx, kn, vn, acc, top,
    s_even, s_odd, p_even, p_odd, f_even, f_odd, back_send, back_recv,
    w_sem, hs_sem, hr_sem, qs_sem, qr_sem, zs_sem, zr_sem, ys_sem, yr_sem, rs_sem, rr_sem, ls_sem, lr_sem, bs_sem, br_sem,
):
    lat = lax.axis_index("lat")
    lon = lax.axis_index("lon")
    z = lon // ny
    y = lon % ny
    nlon = nz * ny
    width = nz * LANES
    has_north = lat > 0
    has_south = lat < nlat - 1

    def wrap(i, n):
        return lax.rem(i + n, n)

    def at(zz, yy):
        return (lat, zz * ny + yy)

    wq_copy = pltpu.make_async_copy(w_qkv, wq, w_sem.at[0])
    wo_copy = pltpu.make_async_copy(w_out, wo, w_sem.at[1])
    wq_copy.start()
    wo_copy.start()

    barrier = pltpu.get_barrier_semaphore()

    def greet(dev):
        pl.semaphore_signal(barrier, inc=1, device_id=dev, device_id_type=MESH)

    for k in range(1, nz):
        greet(at(wrap(z + k, nz), y))
    greet(at(z, wrap(y + 1, ny)))
    greet(at(z, wrap(y - 1, ny)))
    greet((lat, wrap(lon + 1, nlon)))
    greet((lat, wrap(lon - 1, nlon)))

    @pl.when(has_north)
    def _():
        for d in (-1, 0, 1):
            greet((lat - 1, wrap(lon + d, nlon)))

    @pl.when(has_south)
    def _():
        for d in (-1, 0, 1):
            greet((lat + 1, wrap(lon + d, nlon)))

    for l in range(LEVELS):
        for c in range(COLS):
            cells = fields[l, c].astype(F32)
            for t in range(nz):
                flat[t, pl.ds((l * COLS + c) * ROWS, ROWS), :] = cells[:, t * LANES : (t + 1) * LANES]
    for r in range(ROWS):
        for c in range(COLS):
            for t in range(nz):
                grid[r + 1, c + 1, 0:LEVELS, t * LANES : (t + 1) * LANES] = flat[
                    t, pl.ds(c * ROWS + r, LEVELS, stride=COLS * ROWS), :
                ]

    def exists(a):
        return {-1: has_north, 0: None, 1: has_south}[a]

    def maybe(cond, fn):
        if cond is None:
            fn()
        else:
            pl.when(cond)(fn)

    def halo_copy(which, i):
        a, b, first, rows = SIDES[i]
        first_there = SIDES[OPPOSITE[i]][2]
        return pltpu.make_async_remote_copy(
            src_ref=halo_send.at[which, pl.ds(first, rows)],
            dst_ref=halo_recv.at[which, pl.ds(first_there, rows)],
            send_sem=hs_sem.at[which, i],
            recv_sem=hr_sem.at[which, OPPOSITE[i]],
            device_id=(lat + a, wrap(lon + b, nlon)),
            device_id_type=MESH,
        )

    def halo_wait(which, i):
        a, b, first, rows = SIDES[i]
        return pltpu.make_async_remote_copy(
            src_ref=halo_send.at[which, pl.ds(first, rows)],
            dst_ref=halo_recv.at[which, pl.ds(first, rows)],
            send_sem=hs_sem.at[which, i],
            recv_sem=hr_sem.at[which, i],
            device_id=(lat + a, wrap(lon + b, nlon)),
            device_id_type=MESH,
        )

    def halo_start(which):
        for i, (a, b, first, rows) in enumerate(SIDES):
            rim, _ = cells_of(a, b)
            for n, (r, c) in enumerate(rim):
                halo_f[pl.ds(first + 4 * n, 4), :] = grid[r, c, 0:LEVELS, :]
            halo_send[which, pl.ds(first, rows), :] = halo_f[pl.ds(first, rows), :].astype(BF16)
            maybe(exists(a), lambda: halo_copy(which, i).start())

    def halo_end(which):
        for i, (a, b, first, rows) in enumerate(SIDES):
            maybe(exists(a), lambda: halo_wait(which, i).wait_recv())
            halo_f[pl.ds(first, rows), :] = halo_recv[which, pl.ds(first, rows), :].astype(F32)
            _, beyond = cells_of(a, b)
            for n, (r, c) in enumerate(beyond):
                value = halo_f[pl.ds(first + 4 * n, 4), :]
                if a != 0:
                    value = jnp.where(exists(a), value, 0.0)
                grid[r, c, 0:LEVELS, :] = value

    def conv(weights, dst):
        chunk = min(256, width)
        for first in range(0, width, chunk):
            lanes = slice(first, first + chunk)
            w = weights[:, lanes]
            for r in range(ROWS):
                total = grid[r + 1, 1 : COLS + 1, 0:LEVELS, lanes]
                for a in range(3):
                    for b in range(3):
                        total = total + w[3 * a + b][None, None, :] * grid[r + a, b : b + COLS, 0:LEVELS, lanes]
                total = total.astype(BF16).astype(F32)
                for c in range(COLS):
                    for t in range(chunk // LANES):
                        dst[first // LANES + t, pl.ds((r * COLS + c) * LEVELS, LEVELS), :] = total[
                            c, :, t * LANES : (t + 1) * LANES
                        ]

    greetings = nz - 1 + 4 + 3 * has_north.astype(jnp.int32) + 3 * has_south.astype(jnp.int32)
    halo_f[...] = jnp.zeros_like(halo_f)
    pl.semaphore_wait(barrier, greetings)
    halo_start(0)

    lane = lax.broadcasted_iota(jnp.int32, (16, LANES), 1)
    count = key_count[0, 0]
    seen = ((lane == nlon) & has_north) | ((lane == nlon + 1) & has_south)
    for s in range(nlon):
        seen = seen | (lane == jnp.where(s < count, key_list[0, 0, s], -1))
    bias = jnp.where(seen, 0.0, NEG).astype(BF16)
    for k in range(nz):
        q_send[k, pl.ds(TOK, 16), :] = bias

    lane_t = lax.broadcasted_iota(jnp.int32, (TOK, LANES), 1)
    ones = jnp.ones((CHUNK, LANES), BF16)
    for u in range(2):
        vx[u, :, LANES:] = ones
        vn[u, :, LANES:] = ones[: 2 * TOK]
        for side in range(2):
            kn[u, pl.ds(side * TOK, TOK), LANES:] = jnp.where(lane_t == nlon + side, 1.0, 0.0).astype(BF16)
    vx[1, :, 0:LANES] = jnp.zeros((CHUNK, LANES), BF16)
    p_odd[...] = jnp.zeros_like(p_odd)
    f_odd[...] = jnp.ones_like(f_odd)

    def clear(o, carry):
        top[o] = jnp.full((2 * TOK, LANES), LOW, F32)
        acc[o] = jnp.zeros((2 * TOK, 2 * LANES), F32)
        return carry

    lax.fori_loop(0, nz, clear, 0)

    @pl.when(jnp.logical_not(has_north))
    def _():
        near[0] = jnp.zeros(near.shape[1:], BF16)

    @pl.when(jnp.logical_not(has_south))
    def _():
        near[1] = jnp.zeros(near.shape[1:], BF16)

    halo_end(0)
    conv(conv_a, stream)

    def tokens(ref):
        return jnp.concatenate([ref[t] for t in range(nz)], axis=1)

    def keep(ref, value):
        for t in range(nz):
            ref[t] = value[:, t * LANES : (t + 1) * LANES]

    x = tokens(stream)
    normed = (x * lax.rsqrt(jnp.mean(x * x, axis=-1, keepdims=True) + EPSILON)).astype(BF16)

    def shift(o):
        odd = o % 2
        return odd * ((o + 1) // 2) + (1 - odd) * ((nz - o // 2) % nz)

    def remote(src, dst, send_sem, recv_sem, dev):
        return pltpu.make_async_remote_copy(
            src_ref=src, dst_ref=dst, send_sem=send_sem, recv_sem=recv_sem, device_id=dev, device_id_type=MESH
        )

    def q_copy(o):
        there = wrap(z + shift(o), nz)
        return remote(q_send.at[there], q_recv.at[o], qs_sem.at[o], qr_sem.at[o], at(there, y))

    def z_copy(o):
        there = wrap(z + shift(o), nz)
        return remote(kv_send.at[there], kv.at[4 * o], zs_sem.at[o], zr_sem.at[o], at(there, y))

    def y_copy(way, o):
        return remote(
            kv.at[4 * o], kv.at[4 * o + 1 + way], ys_sem.at[way, o], yr_sem.at[way, o],
            at(z, wrap(y + 1 - 2 * way, ny)),
        )

    def relay_copy(way, o):
        rows = pl.ds(way * TOK, TOK)
        return remote(
            kv.at[4 * o + 1 + way, rows], kv.at[4 * o + 3, rows], rs_sem.at[way, o], rr_sem.at[way, o],
            at(z, wrap(y + 1 - 2 * way, ny)),
        )

    def lat_copy(way, o):
        return remote(
            kv.at[4 * o], near.at[1 - way, o], ls_sem.at[way, o], lr_sem.at[1 - way, o], (lat - 1 + 2 * way, lon)
        )

    def lat_wait(side, o):
        return remote(kv.at[4 * o], near.at[side, o], ls_sem.at[side, o], lr_sem.at[side, o], (lat - 1 + 2 * side, lon))

    def back_copy(o):
        return remote(
            back_send.at[o], back_recv.at[z], bs_sem.at[o], br_sem.at[o], at(wrap(z - shift(o), nz), y)
        )

    def back_wait(o):
        there = wrap(z + shift(o), nz)
        return remote(back_send.at[o], back_recv.at[there], bs_sem.at[o], br_sem.at[o], at(there, y))

    def project(part, j):
        cols = pl.ds(pl.multiple_of(part * width + j * 256, 256), 256)
        return jnp.dot(normed, wq[:, cols], preferred_element_type=F32)

    scale = HEAD ** -0.5 * math.log2(math.e)
    wq_copy.wait()
    for j in range(nz // 2):
        res = (project(0, j) * scale).astype(BF16)
        q_send[2 * j, pl.ds(0, TOK), :] = res[:, :LANES]
        q_send[2 * j + 1, pl.ds(0, TOK), :] = res[:, LANES:]
    for o in range(1, nz):
        q_copy(o).start()
    for j in range(nz // 2):
        for part in range(2):
            res = project(1 + part, j).astype(BF16)
            kv_send[2 * j, pl.ds(part * TOK, TOK), :] = res[:, :LANES]
            kv_send[2 * j + 1, pl.ds(part * TOK, TOK), :] = res[:, LANES:]
    for o in range(1, nz):
        z_copy(o).start()
    q_recv[0] = q_send[z]
    kv[0] = kv_send[z]

    def forward(o):
        y_copy(0, o).start()
        y_copy(1, o).start()

        @pl.when(has_north)
        def _():
            lat_copy(0, o).start()

        @pl.when(has_south)
        def _():
            lat_copy(1, o).start()

    def relay(o):
        for way in range(2):
            y_copy(way, o).wait_recv()
            relay_copy(way, o).start()

    def relayed(o):
        for way in range(2):
            relay_copy(way, o).wait_recv()

    forward(0)

    def prepare(o, carry):
        @pl.when(o > 0)
        def _():
            q_copy(o).wait_recv()

        q = q_recv[o, pl.ds(0, TOK), :]
        b = jnp.concatenate([q_recv[o, pl.ds(TOK, 16), :]] * (TOK // 16), axis=0)
        zero = jnp.zeros_like(q)
        qx[o, pl.ds(0, TOK), 0:LANES] = jnp.where(lane_t < HEAD, q, zero)
        qx[o, pl.ds(TOK, TOK), 0:LANES] = jnp.where(lane_t < HEAD, zero, q)
        qx[o, pl.ds(0, TOK), LANES:] = b
        qx[o, pl.ds(TOK, TOK), LANES:] = b
        return carry

    def chunk_keys(c, slot):
        keys = jnp.concatenate([kv[8 * c + i, pl.ds(0, TOK), :] for i in range(8)], axis=0)
        kt[slot, 0:LANES, :] = keys.T
        column = lax.broadcasted_iota(jnp.int32, (LANES, CHUNK), 1)
        number = jnp.zeros((LANES, CHUNK), jnp.int32)
        for i in range(8):
            yy = (y, wrap(y - 1, ny), wrap(y + 1, ny), wrap(y + 2, ny))[i % 4]
            here = wrap(z - shift(2 * c + i // 4), nz) * ny + yy
            number = jnp.where(column >= i * TOK, here, number)
        row = lax.broadcasted_iota(jnp.int32, (LANES, CHUNK), 0)
        kt[slot, LANES:, :] = jnp.where(row == number, 1.0, 0.0).astype(BF16)
        for i in range(8):
            vx[slot, pl.ds(i * TOK, TOK), 0:LANES] = kv[8 * c + i, pl.ds(TOK, TOK), :]

    def soften(s, o):
        old = top[o]
        new = jnp.maximum(old, jnp.max(s, axis=1, keepdims=True))
        top[o] = new
        return jnp.exp2(s - new[:, :1]).astype(BF16), jnp.exp2(old - new)

    def gain(o, factor, p, values):
        pv = jnp.dot(p, values, preferred_element_type=F32)
        return acc[o] * jnp.concatenate([factor, factor], axis=1) + pv

    z_copy(1).wait_recv()
    forward(1)
    relay(0)
    lax.fori_loop(0, nz, prepare, 0)
    relay(1)
    relayed(0)
    relayed(1)
    chunk_keys(0, 0)
    chunks = nz // 2
    steps = chunks * nz
    s_even[...] = jnp.dot(qx[0], kt[0], preferred_element_type=F32)
    s_refs, p_refs, f_refs = (s_even, s_odd), (p_even, p_odd), (f_even, f_odd)

    def advance(c, h):
        def act(a, fn):
            pl.when((h == a * (nz // 2) // 4) & (c < chunks - 1))(fn)

        def first():
            z_copy(2 * c + 2).wait_recv()
            forward(2 * c + 2)

        def second():
            z_copy(2 * c + 3).wait_recv()
            forward(2 * c + 3)
            relay(2 * c + 2)

        def third():
            relay(2 * c + 3)

        def fourth():
            relayed(2 * c + 2)
            relayed(2 * c + 3)
            chunk_keys(c + 1, (c + 1) % 2)

        act(0, first)
        act(1, second)
        act(2, third)
        act(3, fourth)

    def pair(t2, carry):
        advance(t2 // (nz // 2), t2 % (nz // 2))
        for u in range(2):
            t = 2 * t2 + u
            s_refs[1 - u][...] = jnp.dot(qx[(t + 1) % nz], kt[((t + 1) // nz) % 2], preferred_element_type=F32)
            p, factor = soften(s_refs[u][...], t % nz)
            before = (t + nz - 1) % nz
            acc[before] = gain(before, f_refs[1 - u][...], p_refs[1 - u][...], vx[((t + nz - 1) // nz + 1) % 2])
            p_refs[u][...] = p
            f_refs[u][...] = factor
        return carry

    lax.fori_loop(0, steps // 2, pair, 0)
    acc[nz - 1] = gain(nz - 1, f_odd[...], p_odd[...], vx[(chunks - 1) % 2])

    def finish(i, carry):
        numbers = [nz - 1 - 2 * i, nz - 2 - 2 * i]
        for u, o in enumerate(numbers):
            for side, cond in ((0, has_north), (1, has_south)):

                @pl.when(cond)
                def _():
                    lat_wait(side, o).wait_recv()

        for u, o in enumerate(numbers):
            for side in range(2):
                rows = pl.ds(side * TOK, TOK)
                kn[u, rows, 0:LANES] = near[side, o, pl.ds(0, TOK), :]
                vn[u, rows, 0:LANES] = near[side, o, pl.ds(TOK, TOK), :]
        scores = [
            lax.dot_general(qx[o], kn[u], (((1,), (1,)), ((), ())), preferred_element_type=F32)
            for u, o in enumerate(numbers)
        ]
        soft = [soften(s, o) for s, o in zip(scores, numbers)]
        for u, o in enumerate(numbers):
            p, factor = soft[u]
            result = gain(o, factor, p, vn[u])
            result = result[:, :LANES] / result[:, LANES:]
            result = jnp.where(lane_t < HEAD, result[:TOK], result[TOK:]).astype(BF16)
            back_send[o] = result

        for u, o in enumerate(numbers):

            @pl.when(o > 0)
            def _():
                back_copy(o).start()

        return carry

    lax.fori_loop(0, nz // 2, finish, 0)
    back_recv[z] = back_send[0]
    for o in range(1, nz):
        back_wait(o).wait_recv()

    attended = jnp.concatenate([back_recv[k] for k in range(nz)], axis=1)
    wo_copy.wait()
    after = tokens(stream) + jnp.dot(attended, wo[...], preferred_element_type=F32)
    keep(stage, after.astype(BF16).astype(F32))
    for r in range(ROWS):
        for c in range(COLS):
            for t in range(nz):
                grid[r + 1, c + 1, 0:LEVELS, t * LANES : (t + 1) * LANES] = stage[
                    t, pl.ds((r * COLS + c) * LEVELS, LEVELS), :
                ]
    halo_start(1)
    keep(stage, attended.astype(F32))

    def leave(out):
        for l in range(LEVELS):
            for c in range(COLS):
                for t in range(nz):
                    out[l, c, :, t * LANES : (t + 1) * LANES] = stage[
                        t, pl.ds(c * LEVELS + l, ROWS, stride=COLS * LEVELS), :
                    ].astype(BF16)

    leave(att_out)
    halo_end(1)
    conv(conv_b, stage)
    leave(mix_out)

    for which in range(2):
        for i, (a, b, first, rows) in enumerate(SIDES):
            maybe(exists(a), lambda: halo_copy(which, i).wait_send())

    def sent(o, carry):
        @pl.when(o > 0)
        def _():
            q_copy(o).wait_send()
            z_copy(o).wait_send()
            back_copy(o).wait_send()

        for way in range(2):
            y_copy(way, o).wait_send()
            relay_copy(way, o).wait_send()

        @pl.when(has_north)
        def _():
            lat_copy(0, o).wait_send()

        @pl.when(has_south)
        def _():
            lat_copy(1, o).wait_send()

        return carry

    lax.fori_loop(0, nz, sent, 0)


def local(nlat, nz, ny, fields, conv_first, w_qkv, w_out, conv_second, key_list, key_count):
    width = fields.shape[-1]
    vmem = pl.BlockSpec(memory_space=pltpu.VMEM)
    smem = pl.BlockSpec(memory_space=pltpu.SMEM)
    hbm = pl.BlockSpec(memory_space=pl.ANY)
    dma = pltpu.SemaphoreType.DMA
    fields = fields.transpose(0, 2, 1, 3)
    out = jax.ShapeDtypeStruct(fields.shape, BF16)
    attended, mixed = pl.pallas_call(
        functools.partial(kernel, nlat, nz, ny),
        out_shape=(out, out),
        in_specs=[vmem, vmem, vmem, smem, smem, hbm, hbm],
        out_specs=(vmem, vmem),
        scratch_shapes=[
            pltpu.VMEM(w_qkv.shape, BF16),
            pltpu.VMEM(w_out.shape, BF16),
            pltpu.VMEM((nz, TOK, LANES), F32),
            pltpu.VMEM((ROWS + 2, COLS + 2, 8, width), F32),
            pltpu.VMEM((nz, TOK, LANES), F32),
            pltpu.VMEM((nz, TOK, LANES), F32),
            pltpu.VMEM((HALO_ROWS, width), F32),
            pltpu.VMEM((2, HALO_ROWS, width), BF16),
            pltpu.VMEM((2, HALO_ROWS, width), BF16),
            pltpu.VMEM((nz, TOK + 16, LANES), BF16),
            pltpu.VMEM((nz, TOK + 16, LANES), BF16),
            pltpu.VMEM((nz, 2 * TOK, LANES), BF16),
            pltpu.VMEM((4 * nz, 2 * TOK, LANES), BF16),
            pltpu.VMEM((2, nz, 2 * TOK, LANES), BF16),
            pltpu.VMEM((nz, 2 * TOK, 2 * LANES), BF16),
            pltpu.VMEM((2, 2 * LANES, CHUNK), BF16),
            pltpu.VMEM((2, CHUNK, 2 * LANES), BF16),
            pltpu.VMEM((2, 2 * TOK, 2 * LANES), BF16),
            pltpu.VMEM((2, 2 * TOK, 2 * LANES), BF16),
            pltpu.VMEM((nz, 2 * TOK, 2 * LANES), F32),
            pltpu.VMEM((nz, 2 * TOK, LANES), F32),
            pltpu.VMEM((2 * TOK, CHUNK), F32),
            pltpu.VMEM((2 * TOK, CHUNK), F32),
            pltpu.VMEM((2 * TOK, CHUNK), BF16),
            pltpu.VMEM((2 * TOK, CHUNK), BF16),
            pltpu.VMEM((2 * TOK, LANES), F32),
            pltpu.VMEM((2 * TOK, LANES), F32),
            pltpu.VMEM((nz, TOK, LANES), BF16),
            pltpu.VMEM((nz, TOK, LANES), BF16),
            dma((2,)),
            dma((2, 8)),
            dma((2, 8)),
            dma((nz,)),
            dma((nz,)),
            dma((nz,)),
            dma((nz,)),
            dma((2, nz)),
            dma((2, nz)),
            dma((2, nz)),
            dma((2, nz)),
            dma((2, nz)),
            dma((2, nz)),
            dma((nz,)),
            dma((nz,)),
        ],
        compiler_params=pltpu.CompilerParams(
            collective_id=0, has_side_effects=True, vmem_limit_bytes=56 * 1024 * 1024
        ),
        name="block",
    )(fields, conv_first, conv_second, key_list, key_count, w_qkv, w_out)
    return attended.transpose(0, 2, 1, 3), mixed.transpose(0, 2, 1, 3)


def solution(mesh):
    nlat, nlon = mesh.shape["lat"], mesh.shape["lon"]
    nz = 8
    return jax.shard_map(
        functools.partial(local, nlat, nz, nlon // nz),
        mesh=mesh,
        in_specs=(
            P(None, "lat", "lon", None),
            P(),
            P(),
            P(),
            P(),
            P("lat", "lon", None),
            P("lat", "lon"),
        ),
        out_specs=(P(None, "lat", "lon", None), P(None, "lat", "lon", None)),
        check_vma=False,
    )
```

time: 120 us -> 96.5 us (0.80)
  Pallas kernels: 113 us -> 91.4 us
  local copies, waits for them, and re-layouts: 5.88 us -> 3.56 us
    pallas_call x1, Pallas kernels: 113 us -> 91.4 us  [local(): pl.pallas_call(functools.partial(kernel, nlat, nz, ny), out_shape=(out, o...]
    pallas_call x2 -> x0, local copies, waits for them, and re-layouts: 4 us -> none  [local(): pl.pallas_call(functools.partial(kernel, nlat, nz, ny), out_shape=(out, o...]
    unnamed x1 -> x2, local copies, waits for them, and re-layouts: 1.88 us -> 3.56 us
where the time goes in v2:
time: 96.5 us; the launch traced here: 96.3 us
  Pallas kernels  91.4 us (95%)
  local copies, waits for them, and re-layouts  3.56 us (4%)
  between operations  1.29 us (1%)
    pallas_call x1, Pallas kernels, local(): pl.pallas_call(functools.partial(kernel, nlat, nz, ny), out_shape=(out, o...  91.4 us
    unnamed x2, local copies, waits for them, and re-layouts  3.56 us

profile of v2, /device:TPU:1, one launch (start us, length us, event | category | flops | bytes accessed | tf_op | source)
XLA Modules:
  0.0 96.3 jit_solution(8024497100785351306)
XLA Ops:
  1.3 91.4 %block.1 = (bf16[4,9,4,1024]{3,2,1,0:T(4,128)(2,1)}, bf16[4,9,4,1024]{3,2,1,0:T(4,128)(2,1)}) custom-call(bf16[4,9,4,1024]{3,2,1,0:T(4,128)(2,1)} %bitcast.3, f32[9,1024]{1,0:T(8,128)} %conv_a.1, f32[9,1024]{1,0:T(8,128)} %conv_b.1, s32[1,1,32]{2,1,0:T(1,128)} %key_list.1, s32[1,1]{1,0:T(1,128)S(6)} %copy.11.key_count, bf16[1024,3072]{1,0:T(8,128)(2,1)} %w_qkv.1, ...), custom_call_target="tpu_custom_call" | custom-call | tf_op jit(solution)/shard_map/block/pallas_call | solution.py:512
  92.7 1.8 %copy.12 = bf16[4,4,9,1024]{3,1,2,0:T(4,128)(2,1)} copy(bf16[4,4,9,1024]{3,1,2,0:T(4,128)(2,1)} %bitcast.5) | data formatting | bytes 589824
  94.5 1.8 %copy.13 = bf16[4,4,9,1024]{3,1,2,0:T(4,128)(2,1)} copy(bf16[4,4,9,1024]{3,1,2,0:T(4,128)(2,1)} %bitcast.4) | data formatting | bytes 589824

commit v3 on v2

--- a/solution.py
+++ b/solution.py
@@ -278,43 +278,49 @@
     scale = HEAD ** -0.5 * math.log2(math.e)
     wq_copy.wait()
     for j in range(nz // 2):
+        for part in range(2):
+            res = project(1 + part, j).astype(BF16)
+            kv_send[2 * j, pl.ds(part * TOK, TOK), :] = res[:, :LANES]
+            kv_send[2 * j + 1, pl.ds(part * TOK, TOK), :] = res[:, LANES:]
+    for o in range(1, 5):
+        z_copy(o).start()
+    kv[0] = kv_send[z]
+
+    def forward(o):
+        y_copy(0, o).start()
+        y_copy(1, o).start()
+
+        @pl.when(has_north)
+        def _():
+            lat_copy(0, o).start()
+
+        @pl.when(has_south)
+        def _():
+            lat_copy(1, o).start()
+
+    def relay(o):
+        for way in range(2):
+            y_copy(way, o).wait_recv()
+            relay_copy(way, o).start()
+
+    def relayed(o):
+        for way in range(2):
+            relay_copy(way, o).wait_recv()
+
+    def arrive(o):
+        z_copy(o).wait_recv()
+        forward(o)
+        if o + 4 < nz:
+            z_copy(o + 4).start()
+
+    forward(0)
+    for j in range(nz // 2):
         res = (project(0, j) * scale).astype(BF16)
         q_send[2 * j, pl.ds(0, TOK), :] = res[:, :LANES]
         q_send[2 * j + 1, pl.ds(0, TOK), :] = res[:, LANES:]
     for o in range(1, nz):
         q_copy(o).start()
-    for j in range(nz // 2):
-        for part in range(2):
-            res = project(1 + part, j).astype(BF16)
-            kv_send[2 * j, pl.ds(part * TOK, TOK), :] = res[:, :LANES]
-            kv_send[2 * j + 1, pl.ds(part * TOK, TOK), :] = res[:, LANES:]
-    for o in range(1, nz):
-        z_copy(o).start()
     q_recv[0] = q_send[z]
-    kv[0] = kv_send[z]
-
-    def forward(o):
-        y_copy(0, o).start()
-        y_copy(1, o).start()
-
-        @pl.when(has_north)
-        def _():
-            lat_copy(0, o).start()
-
-        @pl.when(has_south)
-        def _():
-            lat_copy(1, o).start()
-
-    def relay(o):
-        for way in range(2):
-            y_copy(way, o).wait_recv()
-            relay_copy(way, o).start()
-
-    def relayed(o):
-        for way in range(2):
-            relay_copy(way, o).wait_recv()
-
-    forward(0)
 
     def prepare(o, carry):
         @pl.when(o > 0)
@@ -354,47 +360,58 @@
         pv = jnp.dot(p, values, preferred_element_type=F32)
         return acc[o] * jnp.concatenate([factor, factor], axis=1) + pv
 
-    z_copy(1).wait_recv()
-    forward(1)
+    chunks = nz // 2
+    steps = chunks * nz
+    half = nz // 2
+    arrive(1)
     relay(0)
-    lax.fori_loop(0, nz, prepare, 0)
+    arrive(2)
     relay(1)
+    prepare(0, 0)
     relayed(0)
     relayed(1)
     chunk_keys(0, 0)
-    chunks = nz // 2
-    steps = chunks * nz
-    s_even[...] = jnp.dot(qx[0], kt[0], preferred_element_type=F32)
+    if nz > 4:
+        plan = {
+            0: [(arrive, 3), (relay, 2)],
+            1: [(arrive, 4), (relay, 3)],
+            2: [(arrive, 5)],
+            3: [(relay, 4)],
+            4: [(arrive, 6), (relay, 5)],
+            5: [(arrive, 7)],
+            6: [(relay, 6)],
+            8: [(relay, 7)],
+        }
+        late = []
+    else:
+        plan = {}
+        late = [(relay, 2), (arrive, 3), (relay, 3)]
     s_refs, p_refs, f_refs = (s_even, s_odd), (p_even, p_odd), (f_even, f_odd)
 
-    def advance(c, h):
-        def act(a, fn):
-            pl.when((h == a * (nz // 2) // 4) & (c < chunks - 1))(fn)
-
-        def first():
-            z_copy(2 * c + 2).wait_recv()
-            forward(2 * c + 2)
-
-        def second():
-            z_copy(2 * c + 3).wait_recv()
-            forward(2 * c + 3)
-            relay(2 * c + 2)
-
-        def third():
-            relay(2 * c + 3)
-
-        def fourth():
+    def advance(t2):
+        for when, acts in plan.items():
+
+            @pl.when(t2 == when)
+            def _():
+                for fn, o in acts:
+                    fn(o)
+
+        c = t2 // half
+
+        @pl.when((t2 % half == half - 1) & (c < chunks - 2))
+        def _():
             relayed(2 * c + 2)
             relayed(2 * c + 3)
             chunk_keys(c + 1, (c + 1) % 2)
 
-        act(0, first)
-        act(1, second)
-        act(2, third)
-        act(3, fourth)
-
     def pair(t2, carry):
-        advance(t2 // (nz // 2), t2 % (nz // 2))
+        for i in (1, 2):
+
+            @pl.when(2 * t2 + i < nz)
+            def _():
+                prepare(2 * t2 + i, 0)
+
+        advance(t2)
         for u in range(2):
             t = 2 * t2 + u
             s_refs[1 - u][...] = jnp.dot(qx[(t + 1) % nz], kt[((t + 1) // nz) % 2], preferred_element_type=F32)
@@ -405,11 +422,15 @@
             f_refs[u][...] = factor
         return carry
 
-    lax.fori_loop(0, steps // 2, pair, 0)
-    acc[nz - 1] = gain(nz - 1, f_odd[...], p_odd[...], vx[(chunks - 1) % 2])
-
-    def finish(i, carry):
-        numbers = [nz - 1 - 2 * i, nz - 2 - 2 * i]
+    s_even[...] = jnp.dot(qx[0], kt[0], preferred_element_type=F32)
+    lax.fori_loop(0, (chunks - 1) * half, pair, 0)
+    acc[nz - 1] = gain(nz - 1, f_odd[...], p_odd[...], vx[(chunks - 2) % 2])
+    last = chunks - 1
+    for fn, o in late:
+        fn(o)
+
+    def beside(i, carry):
+        numbers = [2 * i, 2 * i + 1]
         for u, o in enumerate(numbers):
             for side, cond in ((0, has_north), (1, has_south)):
 
@@ -429,21 +450,43 @@
         soft = [soften(s, o) for s, o in zip(scores, numbers)]
         for u, o in enumerate(numbers):
             p, factor = soft[u]
-            result = gain(o, factor, p, vn[u])
-            result = result[:, :LANES] / result[:, LANES:]
-            result = jnp.where(lane_t < HEAD, result[:TOK], result[TOK:]).astype(BF16)
-            back_send[o] = result
-
-        for u, o in enumerate(numbers):
-
-            @pl.when(o > 0)
+            acc[o] = gain(o, factor, p, vn[u])
+        return carry
+
+    lax.fori_loop(0, nz // 2, beside, 0)
+
+    relayed(2 * last)
+    relayed(2 * last + 1)
+    chunk_keys(last, last % 2)
+    keys_last, values_last = kt.at[last % 2], vx.at[last % 2]
+    p_odd[...] = jnp.zeros_like(p_odd)
+    f_odd[...] = jnp.ones_like(f_odd)
+
+    def result(o, factor, p):
+        total = gain(o, factor, p, values_last[...])
+        total = total[:, :LANES] / total[:, LANES:]
+        return jnp.where(lane_t < HEAD, total[:TOK], total[TOK:]).astype(BF16)
+
+    def finish(i2, carry):
+        for u in range(2):
+            i = 2 * i2 + u
+            o = nz - 1 - i
+            s_refs[1 - u][...] = jnp.dot(qx[(o + nz - 1) % nz], keys_last[...], preferred_element_type=F32)
+            p, factor = soften(s_refs[u][...], o)
+            before = (o + 1) % nz
+            back_send[before] = result(before, f_refs[1 - u][...], p_refs[1 - u][...])
+            p_refs[u][...] = p
+            f_refs[u][...] = factor
+
+            @pl.when(i > 0)
             def _():
-                back_copy(o).start()
+                back_copy(before).start()
 
         return carry
 
-    lax.fori_loop(0, nz // 2, finish, 0)
-    back_recv[z] = back_send[0]
+    s_even[...] = jnp.dot(qx[nz - 1], keys_last[...], preferred_element_type=F32)
+    lax.fori_loop(0, half, finish, 0)
+    back_recv[z] = result(0, f_odd[...], p_odd[...])
     for o in range(1, nz):
         back_wait(o).wait_recv()
 

time: 96.5 us -> 83.6 us (0.87)
  Pallas kernels: 91.4 us -> 78.5 us
    pallas_call x1, Pallas kernels: 91.4 us -> 78.5 us  [local(): pl.pallas_call(functools.partial(kernel, nlat, nz, ny), out_shape=(out, o...]
where the time goes in v3:
time: 83.6 us; the launch traced here: 83.4 us
  Pallas kernels  78.5 us (94%)
  local copies, waits for them, and re-layouts  3.56 us (4%)
  between operations  1.29 us (2%)
    pallas_call x1, Pallas kernels, local(): pl.pallas_call(functools.partial(kernel, nlat, nz, ny), out_shape=(out, o...  78.5 us
    unnamed x2, local copies, waits for them, and re-layouts  3.56 us

profile of v3, /device:TPU:1, one launch (start us, length us, event | category | flops | bytes accessed | tf_op | source)
XLA Modules:
  0.0 83.4 jit_solution(9720467032030116975)
XLA Ops:
  1.3 78.5 %block.1 = (bf16[4,9,4,1024]{3,2,1,0:T(4,128)(2,1)}, bf16[4,9,4,1024]{3,2,1,0:T(4,128)(2,1)}) custom-call(bf16[4,9,4,1024]{3,2,1,0:T(4,128)(2,1)} %bitcast.3, f32[9,1024]{1,0:T(8,128)} %conv_a.1, f32[9,1024]{1,0:T(8,128)} %conv_b.1, s32[1,1,32]{2,1,0:T(1,128)} %key_list.1, s32[1,1]{1,0:T(1,128)S(6)} %copy.11.key_count, bf16[1024,3072]{1,0:T(8,128)(2,1)} %w_qkv.1, ...), custom_call_target="tpu_custom_call" | custom-call | tf_op jit(solution)/shard_map/block/pallas_call | solution.py:555
  79.8 1.8 %copy.12 = bf16[4,4,9,1024]{3,1,2,0:T(4,128)(2,1)} copy(bf16[4,4,9,1024]{3,1,2,0:T(4,128)(2,1)} %bitcast.5) | data formatting | bytes 589824
  81.6 1.8 %copy.13 = bf16[4,4,9,1024]{3,1,2,0:T(4,128)(2,1)} copy(bf16[4,4,9,1024]{3,1,2,0:T(4,128)(2,1)} %bitcast.4) | data formatting | bytes 589824

commit v4 on v3

--- a/solution.py
+++ b/solution.py
@@ -13,6 +13,7 @@
 HEAD = 64
 LANES = 128
 CHUNK = 8 * TOK
+MARKS = 48
 EPSILON = 1e-05
 NEG = -1e30
 LOW = -3e38
@@ -188,6 +189,7 @@
     lane_t = lax.broadcasted_iota(jnp.int32, (TOK, LANES), 1)
     ones = jnp.ones((CHUNK, LANES), BF16)
     for u in range(2):
+        kt[u, LANES + MARKS :, :] = jnp.zeros((LANES - MARKS, CHUNK), BF16)
         vx[u, :, LANES:] = ones
         vn[u, :, LANES:] = ones[: 2 * TOK]
         for side in range(2):
@@ -339,14 +341,14 @@
     def chunk_keys(c, slot):
         keys = jnp.concatenate([kv[8 * c + i, pl.ds(0, TOK), :] for i in range(8)], axis=0)
         kt[slot, 0:LANES, :] = keys.T
-        column = lax.broadcasted_iota(jnp.int32, (LANES, CHUNK), 1)
-        number = jnp.zeros((LANES, CHUNK), jnp.int32)
+        column = lax.broadcasted_iota(jnp.int32, (1, CHUNK), 1)
+        number = jnp.zeros((1, CHUNK), jnp.int32)
         for i in range(8):
             yy = (y, wrap(y - 1, ny), wrap(y + 1, ny), wrap(y + 2, ny))[i % 4]
             here = wrap(z - shift(2 * c + i // 4), nz) * ny + yy
             number = jnp.where(column >= i * TOK, here, number)
-        row = lax.broadcasted_iota(jnp.int32, (LANES, CHUNK), 0)
-        kt[slot, LANES:, :] = jnp.where(row == number, 1.0, 0.0).astype(BF16)
+        row = lax.broadcasted_iota(jnp.int32, (MARKS, CHUNK), 0)
+        kt[slot, LANES : LANES + MARKS, :] = jnp.where(row == number, 1.0, 0.0).astype(BF16)
         for i in range(8):
             vx[slot, pl.ds(i * TOK, TOK), 0:LANES] = kv[8 * c + i, pl.ds(TOK, TOK), :]
 
@@ -542,6 +544,11 @@
         return carry
 
     lax.fori_loop(0, nz, sent, 0)
+
+
+def place(attended, mixed, att_out, mix_out):
+    att_out[...] = attended[...]
+    mix_out[...] = mixed[...]
 
 
 def local(nlat, nz, ny, fields, conv_first, w_qkv, w_out, conv_second, key_list, key_count):
@@ -608,6 +615,13 @@
         ),
         name="block",
     )(fields, conv_first, conv_second, key_list, key_count, w_qkv, w_out)
+    attended, mixed = pl.pallas_call(
+        place,
+        out_shape=(out, out),
+        in_specs=[vmem, vmem],
+        out_specs=(vmem, vmem),
+        name="place",
+    )(attended, mixed)
     return attended.transpose(0, 2, 1, 3), mixed.transpose(0, 2, 1, 3)
 
 

time: 83.6 us -> 81.9 us (0.980)
  local copies, waits for them, and re-layouts: 3.56 us -> 0 us
  Pallas kernels: 78.5 us -> 80.4 us
    unnamed x2 -> x0, local copies, waits for them, and re-layouts: 3.56 us -> none
    pallas_call x0 -> x1, Pallas kernels: none -> 1.88 us  [local(): pl.pallas_call(place, out_shape=(out, out), in_specs=[vmem, vmem], out_sp...]
where the time goes in v4:
time: 81.9 us; the launch traced here: 81.7 us
  Pallas kernels  80.4 us (98%)
  between operations  1.29 us (2%)
    pallas_call x1, Pallas kernels, local(): pl.pallas_call(functools.partial(kernel, nlat, nz, ny), out_shape=(out, o...  78.6 us
    pallas_call x1, Pallas kernels, local(): pl.pallas_call(place, out_shape=(out, out), in_specs=[vmem, vmem], out_sp...  1.88 us

profile of v4, /device:TPU:1, one launch (start us, length us, event | category | flops | bytes accessed | tf_op | source)
XLA Modules:
  0.0 81.7 jit_solution(15200289329781470060)
XLA Ops:
  1.3 78.6 %block.1 = (bf16[4,9,4,1024]{3,2,1,0:T(4,128)(2,1)}, bf16[4,9,4,1024]{3,2,1,0:T(4,128)(2,1)}) custom-call(bf16[4,9,4,1024]{3,2,1,0:T(4,128)(2,1)} %bitcast.3, f32[9,1024]{1,0:T(8,128)} %conv_a.1, f32[9,1024]{1,0:T(8,128)} %conv_b.1, s32[1,1,32]{2,1,0:T(1,128)} %key_list.1, s32[1,1]{1,0:T(1,128)S(6)} %copy.9.key_count, bf16[1024,3072]{1,0:T(8,128)(2,1)} %w_qkv.1, ...), custom_call_target="tpu_custom_call" | custom-call | tf_op jit(solution)/shard_map/block/pallas_call | solution.py:562
  79.8 1.9 %place.1 = (bf16[4,9,4,1024]{3,2,1,0:T(4,128)(2,1)}, bf16[4,9,4,1024]{3,2,1,0:T(4,128)(2,1)}) custom-call(bf16[4,9,4,1024]{3,2,1,0:T(4,128)(2,1)} %get-tuple-element.6.attended, bf16[4,9,4,1024]{3,2,1,0:T(4,128)(2,1)} %get-tuple-element.7.mixed), custom_call_target="tpu_custom_call" | custom-call | tf_op jit(solution)/shard_map/place/pallas_call | solution.py:618

commit v5 on v4

--- a/solution.py
+++ b/solution.py
@@ -43,9 +43,9 @@
 
 def kernel(
     nlat, nz, ny,
-    fields, conv_a, conv_b, key_list, key_count, w_qkv, w_out,
+    fields_in, conv_a_in, conv_b_in, key_list, key_count, w_qkv, w_out,
     att_out, mix_out,
-    wq, wo, flat, grid, stream, stage, halo_f, halo_send, halo_recv,
+    fields, conv_a, conv_b, wq, wo, flat, grid, stream, stage, halo_f, halo_send, halo_recv,
     q_send, q_recv, kv_send, kv, near, qx, kt, vx, kn, vn, acc, top,
     s_even, s_odd, p_even, p_odd, f_even, f_odd, back_send, back_recv,
     w_sem, hs_sem, hr_sem, qs_sem, qr_sem, zs_sem, zr_sem, ys_sem, yr_sem, rs_sem, rr_sem, ls_sem, lr_sem, bs_sem, br_sem,
@@ -65,6 +65,12 @@
     def at(zz, yy):
         return (lat, zz * ny + yy)
 
+    fields_copy = pltpu.make_async_copy(fields_in, fields, w_sem.at[2])
+    conv_a_copy = pltpu.make_async_copy(conv_a_in, conv_a, w_sem.at[3])
+    conv_b_copy = pltpu.make_async_copy(conv_b_in, conv_b, w_sem.at[4])
+    fields_copy.start()
+    conv_a_copy.start()
+    conv_b_copy.start()
     wq_copy = pltpu.make_async_copy(w_qkv, wq, w_sem.at[0])
     wo_copy = pltpu.make_async_copy(w_out, wo, w_sem.at[1])
     wq_copy.start()
@@ -92,6 +98,7 @@
         for d in (-1, 0, 1):
             greet((lat + 1, wrap(lon + d, nlon)))
 
+    fields_copy.wait()
     for l in range(LEVELS):
         for c in range(COLS):
             cells = fields[l, c].astype(F32)
@@ -214,6 +221,7 @@
         near[1] = jnp.zeros(near.shape[1:], BF16)
 
     halo_end(0)
+    conv_a_copy.wait()
     conv(conv_a, stream)
 
     def tokens(ref):
@@ -515,6 +523,7 @@
 
     leave(att_out)
     halo_end(1)
+    conv_b_copy.wait()
     conv(conv_b, stage)
     leave(mix_out)
 
@@ -562,9 +571,12 @@
     attended, mixed = pl.pallas_call(
         functools.partial(kernel, nlat, nz, ny),
         out_shape=(out, out),
-        in_specs=[vmem, vmem, vmem, smem, smem, hbm, hbm],
+        in_specs=[hbm, hbm, hbm, smem, smem, hbm, hbm],
         out_specs=(vmem, vmem),
         scratch_shapes=[
+            pltpu.VMEM(fields.shape, BF16),
+            pltpu.VMEM(conv_first.shape, F32),
+            pltpu.VMEM(conv_second.shape, F32),
             pltpu.VMEM(w_qkv.shape, BF16),
             pltpu.VMEM(w_out.shape, BF16),
             pltpu.VMEM((nz, TOK, LANES), F32),
@@ -594,7 +606,7 @@
             pltpu.VMEM((2 * TOK, LANES), F32),
             pltpu.VMEM((nz, TOK, LANES), BF16),
             pltpu.VMEM((nz, TOK, LANES), BF16),
-            dma((2,)),
+            dma((5,)),
             dma((2, 8)),
             dma((2, 8)),
             dma((nz,)),

time: 81.9 us -> 81.9 us (level)
  no operation moved by 1% of the time
where the time goes in v5:
time: 81.9 us; the launch traced here: 81.8 us
  Pallas kernels  80.5 us (98%)
  between operations  1.29 us (2%)
    pallas_call x1, Pallas kernels, local(): pl.pallas_call(functools.partial(kernel, nlat, nz, ny), out_shape=(out, o...  78.6 us
    pallas_call x1, Pallas kernels, local(): pl.pallas_call(place, out_shape=(out, out), in_specs=[vmem, vmem], out_sp...  1.88 us

profile of v5, /device:TPU:1, one launch (start us, length us, event | category | flops | bytes accessed | tf_op | source)
XLA Modules:
  0.0 81.8 jit_solution(11262095584932752901)
XLA Ops:
  1.3 78.6 %block.1 = (bf16[4,9,4,1024]{3,2,1,0:T(4,128)(2,1)}, bf16[4,9,4,1024]{3,2,1,0:T(4,128)(2,1)}) custom-call(bf16[4,9,4,1024]{3,2,1,0:T(4,128)(2,1)} %bitcast.3, f32[9,1024]{1,0:T(8,128)} %conv_a_in.1, f32[9,1024]{1,0:T(8,128)} %conv_b_in.1, s32[1,1,32]{2,1,0:T(1,128)} %key_list.1, s32[1,1]{1,0:T(1,128)S(6)} %copy.9.key_count, bf16[1024,3072]{1,0:T(8,128)(2,1)} %w_qkv.1, ...), custom_call_target="tpu_custom_call" | custom-call | tf_op jit(solution)/shard_map/block/pallas_call | solution.py:571
  79.9 1.9 %place.1 = (bf16[4,9,4,1024]{3,2,1,0:T(4,128)(2,1)}, bf16[4,9,4,1024]{3,2,1,0:T(4,128)(2,1)}) custom-call(bf16[4,9,4,1024]{3,2,1,0:T(4,128)(2,1)} %get-tuple-element.6.attended, bf16[4,9,4,1024]{3,2,1,0:T(4,128)(2,1)} %get-tuple-element.7.mixed), custom_call_target="tpu_custom_call" | custom-call | tf_op jit(solution)/shard_map/place/pallas_call | solution.py:630
